TPU v7x, 128 devices: a whole 4x4x4 slice. The times are simulated.
128 devices in a mesh: group: 8 (over y, z_lo), dev: 16 (over z_hi, x, core).
Axes of the slice: x: 4, y: 4, z: 4 (z_hi: 2, z_lo: 2; z = z_hi * 2 + z_lo), core: 2. Of those that a mesh axis runs over, the one named last changes fastest.
Arguments:
- member_pressure_heads: float32 [192, 512, 768], P('group', 'dev'), may hold values from -4 to 1
- soil_index: int32 [512, 768], P('dev'), may hold values from 0 to 7
- ks_table: float32 [8], replicated, may hold values from 0.05 to 0.5
- alpha_table: float32 [8], replicated, may hold values from 0.5 to 3
- obs_op: float32 [512, 6, 32, 128], P(('dev', 'group')), may hold values from -0.09375 to 0.09375
- obs_mask: int32 [512, 6], P(('dev', 'group')), may hold values from 0 to 1
- obs_values: float32 [512, 6, 32], P(('dev', 'group')), may hold values from -6 to 6
Outputs:
- analysis: float32 [192, 512, 768], P('group', 'dev')
All inputs are finite; a program needn't handle non-finite values.
Results may differ from a plain program's by a relative error of at most 0.0003.
Values sent between devices are 32-bit elements; how exact they have to be, the bound alone decides.
No kernel may reach another device: no remote copies, remote signals or barrier semaphores. Data moves between devices by JAX's collectives and lax.ppermute only.
A program may use at most 64 MiB of HBM per device.

v0:
```python
import jax
import jax.numpy as jnp
from jax import lax
from jax.sharding import PartitionSpec as P

MEMBERS = 192
SOIL_TYPES = 8
MODEL_STEPS = 3
NEWTON_STEPS = 12
BLOCKS = 6


step_duration = 0.1
gravity_head = 1.0
highest = lax.Precision.HIGHEST


def padded(cells, sides, width):
    for axis, dim in sides:
        count = lax.axis_size(axis)
        ends = count - 1
        head = lax.slice_in_dim(cells, 0, width, axis=dim)
        tail = lax.slice_in_dim(cells, cells.shape[dim] - width, cells.shape[dim], axis=dim)
        cells = jnp.concatenate(
            [
                lax.ppermute(tail, axis, [(i, (i + 1) % count) for i in range(ends)]),
                cells,
                lax.ppermute(head, axis, [((i + 1) % count, i) for i in range(ends)]),
            ],
            axis=dim,
        )
    return cells


def soil_values(soil_index, ks_table, alpha_table):
    soil_kinds = jnp.arange(SOIL_TYPES, dtype=jnp.int32)
    one_hot = (soil_index[None] == soil_kinds[:, None, None]).astype(jnp.float32)
    hydraulic_conductance = jnp.sum(one_hot * ks_table[:, None, None], axis=0)
    retention_shape = jnp.sum(one_hot * alpha_table[:, None, None], axis=0)
    return (hydraulic_conductance, retention_shape)


def soil_hydraulic_law(heads_now, hydraulic_conductance, retention_shape):
    factor = jnp.exp(retention_shape * jnp.minimum(heads_now, 0.0))
    return (hydraulic_conductance * factor, 0.1 + 0.4 * retention_shape * factor)


def surface_recharge(padded_heads, padded_k):
    middle = padded_heads[:, 1:-1]
    k_middle = padded_k[:, 1:-1]
    across = 0.5 * (k_middle + padded_k[:, 2:]) * (padded_heads[:, 2:] - middle)
    across = across + 0.5 * (k_middle + padded_k[:, :-2]) * (padded_heads[:, :-2] - middle)
    k_face = 0.5 * (k_middle[..., 1:] + k_middle[..., :-1])
    vertical = k_face * (middle[..., 1:] - middle[..., :-1] - gravity_head)
    border = jnp.zeros_like(middle[..., :1])
    return (
        across + jnp.concatenate([vertical, border], -1) - jnp.concatenate([border, vertical], -1)
    )


def newton_weights(gram_matrix, gram_rhs):
    order_m = gram_matrix.shape[0]
    identity_m = jnp.eye(order_m, dtype=jnp.float32)
    norm_total = jnp.sum(jnp.abs(gram_matrix))

    def one_turn(counter, iterate_pair):
        iterate, inverse = iterate_pair
        middle = 0.5 * (
            3.0 * identity_m
            - jnp.dot(inverse, iterate, precision=highest, preferred_element_type=jnp.float32)
        )
        return (
            jnp.dot(iterate, middle, precision=highest, preferred_element_type=jnp.float32),
            jnp.dot(middle, inverse, precision=highest, preferred_element_type=jnp.float32),
        )

    iterate, inverse = lax.fori_loop(
        0, NEWTON_STEPS, one_turn, (gram_matrix / norm_total, identity_m)
    )
    inner_w = jnp.dot(inverse, gram_rhs, precision=highest, preferred_element_type=jnp.float32)
    shift_w = (
        jnp.dot(inverse, inner_w, precision=highest, preferred_element_type=jnp.float32)
        / norm_total
    )
    return jnp.sqrt((order_m - 1.0) / norm_total) * inverse + shift_w[:, None]


def march_forward(heads_now, hydraulic_conductance, retention_shape):
    for counter in range(MODEL_STEPS):
        conductivity_field, moisture_capacity = soil_hydraulic_law(
            heads_now, hydraulic_conductance, retention_shape
        )
        padded_heads, padded_k = (
            padded(heads_now, (("dev", 1),), 1),
            padded(conductivity_field, (("dev", 1),), 1),
        )
        heads_now = (
            heads_now + step_duration * surface_recharge(padded_heads, padded_k) / moisture_capacity
        )
    return heads_now


def body(member_pressure_heads, soil_index, ks_table, alpha_table, obs_op, obs_mask, obs_values):
    hydraulic_conductance, retention_shape = soil_values(soil_index, ks_table, alpha_table)
    predict_heads = march_forward(member_pressure_heads, hydraulic_conductance, retention_shape)
    mask_float = obs_mask.astype(jnp.float32)
    masked_op = obs_op * mask_float[:, :, None, None]
    masked_values = obs_values * mask_float[:, :, None]
    identity_m = jnp.eye(MEMBERS, dtype=jnp.float32)
    collected_heads = lax.all_to_all(
        predict_heads, "group", split_axis=1, concat_axis=0, tiled=True
    )
    server_rows = collected_heads.shape[1]
    ensemble_average = jnp.sum(collected_heads, axis=0) / MEMBERS
    member_anomalies = collected_heads - ensemble_average
    projected = jnp.einsum(
        "rboc,mrbc->rbom",
        masked_op,
        member_anomalies.reshape(MEMBERS, server_rows, BLOCKS, 128),
        precision=highest,
    ).reshape(-1, MEMBERS)
    innovation = (
        masked_values
        - jnp.einsum(
            "rboc,rbc->rbo",
            masked_op,
            ensemble_average.reshape(server_rows, BLOCKS, 128),
            precision=highest,
        )
    ).reshape(-1)
    gram_part = jnp.dot(
        projected.T, projected, precision=highest, preferred_element_type=jnp.float32
    )
    rhs_part = jnp.dot(
        projected.T, innovation, precision=highest, preferred_element_type=jnp.float32
    )
    gram_total, rhs_total = lax.psum((gram_part, rhs_part), ("group", "dev"))
    mixing = newton_weights(gram_total + (MEMBERS - 1.0) * identity_m, rhs_total)
    mixed = jnp.dot(
        mixing.T,
        member_anomalies.reshape(MEMBERS, -1),
        precision=highest,
        preferred_element_type=jnp.float32,
    )
    analysis = mixed.reshape(collected_heads.shape)
    return lax.all_to_all(analysis, "group", split_axis=0, concat_axis=1, tiled=True)


def solution(mesh):
    placed = (
        P("group", "dev", None),
        P("dev", None),
        P(),
        P(),
        P(("dev", "group"), None, None, None),
        P(("dev", "group"), None),
        P(("dev", "group"), None, None),
    )
    return jax.shard_map(
        body, mesh=mesh, in_specs=placed, out_specs=P("group", "dev", None), check_vma=False
    )
```

profile of v0, /device:TPU:0, one launch (start us, length us, event | category | flops | bytes accessed | tf_op | source)
XLA Modules:
  0.0 337.2 jit_solution(11900502606988095144)
XLA Ops:
  7.6 3.5 %fusion.61 = (f32[24,32,768]{2,0,1:T(8,128)S(1)}, f32[24,32,768]{2,0,1:T(8,128)S(1)}) fusion(f32[32,768]{1,0:T(8,128)S(1)} %get-tuple-element.49, f32[32,768]{1,0:T(8,128)S(1)} %get-tuple-element.48, f32[24,32,768]{2,1,0:T(8,128)} %param.9), kind=kLoop, calls=%fused_computation.84 | loop fusion | flops 1769472 | bytes 7274496 | tf_op jit(solution)/shard_map/mul | solution.py:45
  13.7 3.7 %collective-permute-start.2 = (f32[24,1,768]{2,0,1:T(8,128)S(1)}, f32[24,1,768]{2,0,1:T(8,128)S(1)}, u32[]{:S(2)}, u32[]{:S(2)}) collective-permute-start(f32[24,1,768]{2,0,1:T(8,128)S(1)} %get-tuple-element.71), channel_id=1, source_target_pairs={{0,1},{1,2},{2,3},{3,4},{4,5},{5,6},{6,7},{7,8},{8,9},{9,10},{10,1... | collective-permute-start | bytes 221192 | tf_op jit(solution)/shard_map/ppermute | solution.py:26
  17.4 3.6 %collective-permute-start.3 = (f32[24,1,768]{2,0,1:T(8,128)S(1)}, f32[24,1,768]{2,0,1:T(8,128)S(1)}, u32[]{:S(2)}, u32[]{:S(2)}) collective-permute-start(f32[24,1,768]{2,0,1:T(8,128)S(1)} %get-tuple-element.73), channel_id=1, source_target_pairs={{0,1},{1,2},{2,3},{3,4},{4,5},{5,6},{6,7},{7,8},{8,9},{9,10},{10,1... | collective-permute-start | bytes 221192 | tf_op jit(solution)/shard_map/ppermute | solution.py:26
  22.4 3.1 fusion.60
  28.2 3.7 %collective-permute-start.6 = (f32[24,1,768]{2,0,1:T(8,128)S(1)}, f32[24,1,768]{2,0,1:T(8,128)S(1)}, u32[]{:S(2)}, u32[]{:S(2)}) collective-permute-start(f32[24,1,768]{2,0,1:T(8,128)S(1)} %get-tuple-element.67), channel_id=1, source_target_pairs={{0,1},{1,2},{2,3},{3,4},{4,5},{5,6},{6,7},{7,8},{8,9},{9,10},{10,1... | collective-permute-start | bytes 221192 | tf_op jit(solution)/shard_map/ppermute | solution.py:26
  31.8 3.8 %collective-permute-start.7 = (f32[24,1,768]{2,0,1:T(8,128)S(1)}, f32[24,1,768]{2,0,1:T(8,128)S(1)}, u32[]{:S(2)}, u32[]{:S(2)}) collective-permute-start(f32[24,1,768]{2,0,1:T(8,128)S(1)} %get-tuple-element.69), channel_id=1, source_target_pairs={{0,1},{1,2},{2,3},{3,4},{4,5},{5,6},{6,7},{7,8},{8,9},{9,10},{10,1... | collective-permute-start | bytes 221192 | tf_op jit(solution)/shard_map/ppermute | solution.py:26
  37.0 3.1 fusion.59
  40.1 2.4 collective-permute-start.10
  42.6 4.3 %collective-permute-start.11 = (f32[24,1,768]{2,0,1:T(8,128)S(1)}, f32[24,1,768]{2,0,1:T(8,128)S(1)}, u32[]{:S(2)}, u32[]{:S(2)}) collective-permute-start(f32[24,1,768]{2,0,1:T(8,128)S(1)} %get-tuple-element.65), channel_id=1, source_target_pairs={{0,1},{1,2},{2,3},{3,4},{4,5},{5,6},{6,7},{7,8},{8,9},{9,10},{10,1... | collective-permute-start | bytes 221192 | tf_op jit(solution)/shard_map/ppermute | solution.py:26
  51.9 3.5 %fusion.16 = f32[24,32,768]{2,0,1:T(8,128)} fusion(f32[24,32,768]{2,0,1:T(8,128)S(1)} %get-tuple-element.57, f32[24,1,768]{2,0,1:T(8,128)S(1)} %collective-permute-done.11, f32[24,32,768]{2,0,1:T(8,128)S(1)} %get-tuple-element.56, f32[24,1,768]{2,0,1:T(8,128)S(1)} %collective-permute-done.10, f32[24,1,768]{2,0,1:T(8,128)S(1)} %collective-permute-done.9, ...), kind=kLoop, calls=%fused_computation.21 | loop fusion | flops 12976128 | bytes 9925632 | tf_op jit(solution)/shard_map/add | solution.py:98
  55.5 6.0 %all-to-all-start = ((f32[24,32,768]{2,0,1:T(8,128)}), f32[24,32,768]{2,0,1:T(8,128)S(1)}, u32[]{:S(2)}, u32[]{:S(2)}) async-start(f32[24,32,768]{2,0,1:T(8,128)} %fusion.16), calls=%async_computation | async-start | bytes 4718592 | tf_op jit(solution)/shard_map/all_to_all | solution.py:110
  61.9 33.3 %all-to-all-done = f32[24,32,768]{2,0,1:T(8,128)S(1)} async-done(((f32[24,32,768]{2,0,1:T(8,128)}), f32[24,32,768]{2,0,1:T(8,128)S(1)}, u32[]{:S(2)}, u32[]{:S(2)}) %all-to-all-start) | async-done | bytes 2359328 | tf_op jit(solution)/shard_map/all_to_all | solution.py:110
  96.6 2.7 copy.80
  100.4 1.8 copy.52
  102.2 3.8 %all_to_all.31 = f32[192,4,6,128]{3,2,0,1:T(8,128)} reshape(f32[8,24,4,768]{3,1,0,2:T(8,128)} %copy.52) | data formatting | bytes 4718592 | tf_op jit(solution)/shard_map/all_to_all | solution.py:110
  106.0 2.1 broadcast_subtract_fusion
  108.1 4.3 %fusion.57 = f32[4,6,32,192]{3,2,1,0:T(8,128)S(1)} fusion(f32[192,4,6,128]{3,2,0,1:T(8,128)S(1)} %broadcast_subtract_fusion, f32[4,6,32,128]{3,2,1,0:T(8,128)S(1)} %copy-done.2, f32[4,6]{1,0:T(4,128)S(1)} %convert_element_type.10), kind=kOutput, calls=%fused_computation.77 | convolution fusion | flops 226590720 | bytes 3342432 | tf_op jit(solution)/shard_map/rboc,mrbc->rbom/dot_general | solution.py:116
  113.4 2.1 convolution_bitcast_fusion.1
  116.7 79.0 %psum.15 = f32[192]{0:T(256)S(1)} all-reduce(f32[192]{0:T(256)S(1)} %bitcast.78), channel_id=1, replica_groups=mesh['group'=8,'dev'=16] {'group','dev'}, use_global_device_ids=true, to_apply=%region_7.0 | all-reduce | flops 192 | bytes 1536 | tf_op jit(solution)/shard_map/psum | solution.py:137
  195.7 74.7 %all-reduce.8.cloned.1.call-done = f32[192,192]{1,0:T(8,128)} async-done(((f32[192,192]{1,0:T(8,128)}), f32[192,192]{1,0:T(8,128)}) %all-reduce.8.cloned.1.call-update) | async-done | bytes 147472 | tf_op jit(solution)/shard_map/psum | solution.py:137
  273.7 15.9 %while.13 = (s32[]{:T(128)}, f32[192,192]{0,1:T(8,128)S(1)}, f32[192,192]{1,0:T(8,128)S(1)}, s32[]{:T(128)}) while((s32[]{:T(128)}, f32[192,192]{0,1:T(8,128)S(1)}, f32[192,192]{1,0:T(8,128)S(1)}, s32[]{:T(128)}) %tuple.37), condition=%wide.region_6.0_spmd.clone, body=%wide.region_5.0_spmd.clone.sunk | while | flops 254951424 | bytes 1916981 | solution.py:77
  291.6 2.3 fusion.3
  295.4 32.5 %all_to_all.39 = f32[192,4,768]{2,1,0:T(4,128)S(1)} all-to-all(f32[192,4,768]{2,1,0:T(4,128)S(1)} %copy.59), channel_id=1, replica_groups=mesh['group'=8,'dev'=16] {'group'}, dimensions={0} | all-to-all | bytes 4718592 | tf_op jit(solution)/shard_map/all_to_all | solution.py:146
  328.5 1.9 all_to_all.36
  (124 shorter events, 40.9 us)
Async XLA Ops:
  11.1 11.3 %collective-permute-start = (f32[24,1,768]{2,0,1:T(8,128)S(1)}, f32[24,1,768]{2,0,1:T(8,128)S(1)}, u32[]{:S(2)}, u32[]{:S(2)}) collective-permute-start(f32[24,1,768]{2,0,1:T(8,128)S(1)} %get-tuple-element.70), channel_id=1, source_target_pairs={{1,0},{2,1},{3,2},{4,3},{5,4},{6,5},{7,6},{8,7},{9,8},{10,9},{11,1... | collective-permute-start | bytes 221192 | tf_op jit(solution)/shard_map/ppermute | solution.py:28
  12.4 9.9 %collective-permute-start.1 = (f32[24,1,768]{2,0,1:T(8,128)S(1)}, f32[24,1,768]{2,0,1:T(8,128)S(1)}, u32[]{:S(2)}, u32[]{:S(2)}) collective-permute-start(f32[24,1,768]{2,0,1:T(8,128)S(1)} %get-tuple-element.72), channel_id=1, source_target_pairs={{1,0},{2,1},{3,2},{4,3},{5,4},{6,5},{7,6},{8,7},{9,8},{10,9},{11,1... | collective-permute-start | bytes 221192 | tf_op jit(solution)/shard_map/ppermute | solution.py:28
  13.7 8.7 %collective-permute-start.2 = (f32[24,1,768]{2,0,1:T(8,128)S(1)}, f32[24,1,768]{2,0,1:T(8,128)S(1)}, u32[]{:S(2)}, u32[]{:S(2)}) collective-permute-start(f32[24,1,768]{2,0,1:T(8,128)S(1)} %get-tuple-element.71), channel_id=1, source_target_pairs={{0,1},{1,2},{2,3},{3,4},{4,5},{5,6},{6,7},{7,8},{8,9},{9,10},{10,1... | collective-permute-start | bytes 221192 | tf_op jit(solution)/shard_map/ppermute | solution.py:26
  17.4 5.0 %collective-permute-start.3 = (f32[24,1,768]{2,0,1:T(8,128)S(1)}, f32[24,1,768]{2,0,1:T(8,128)S(1)}, u32[]{:S(2)}, u32[]{:S(2)}) collective-permute-start(f32[24,1,768]{2,0,1:T(8,128)S(1)} %get-tuple-element.73), channel_id=1, source_target_pairs={{0,1},{1,2},{2,3},{3,4},{4,5},{5,6},{6,7},{7,8},{8,9},{9,10},{10,1... | collective-permute-start | bytes 221192 | tf_op jit(solution)/shard_map/ppermute | solution.py:26
  25.5 11.4 %collective-permute-start.4 = (f32[24,1,768]{2,0,1:T(8,128)S(1)}, f32[24,1,768]{2,0,1:T(8,128)S(1)}, u32[]{:S(2)}, u32[]{:S(2)}) collective-permute-start(f32[24,1,768]{2,0,1:T(8,128)S(1)} %get-tuple-element.66), channel_id=1, source_target_pairs={{1,0},{2,1},{3,2},{4,3},{5,4},{6,5},{7,6},{8,7},{9,8},{10,9},{11,1... | collective-permute-start | bytes 221192 | tf_op jit(solution)/shard_map/ppermute | solution.py:28
  26.9 10.1 %collective-permute-start.5 = (f32[24,1,768]{2,0,1:T(8,128)S(1)}, f32[24,1,768]{2,0,1:T(8,128)S(1)}, u32[]{:S(2)}, u32[]{:S(2)}) collective-permute-start(f32[24,1,768]{2,0,1:T(8,128)S(1)} %get-tuple-element.68), channel_id=1, source_target_pairs={{1,0},{2,1},{3,2},{4,3},{5,4},{6,5},{7,6},{8,7},{9,8},{10,9},{11,1... | collective-permute-start | bytes 221192 | tf_op jit(solution)/shard_map/ppermute | solution.py:28
  28.2 8.8 %collective-permute-start.6 = (f32[24,1,768]{2,0,1:T(8,128)S(1)}, f32[24,1,768]{2,0,1:T(8,128)S(1)}, u32[]{:S(2)}, u32[]{:S(2)}) collective-permute-start(f32[24,1,768]{2,0,1:T(8,128)S(1)} %get-tuple-element.67), channel_id=1, source_target_pairs={{0,1},{1,2},{2,3},{3,4},{4,5},{5,6},{6,7},{7,8},{8,9},{9,10},{10,1... | collective-permute-start | bytes 221192 | tf_op jit(solution)/shard_map/ppermute | solution.py:26
  31.8 5.1 %collective-permute-start.7 = (f32[24,1,768]{2,0,1:T(8,128)S(1)}, f32[24,1,768]{2,0,1:T(8,128)S(1)}, u32[]{:S(2)}, u32[]{:S(2)}) collective-permute-start(f32[24,1,768]{2,0,1:T(8,128)S(1)} %get-tuple-element.69), channel_id=1, source_target_pairs={{0,1},{1,2},{2,3},{3,4},{4,5},{5,6},{6,7},{7,8},{8,9},{9,10},{10,1... | collective-permute-start | bytes 221192 | tf_op jit(solution)/shard_map/ppermute | solution.py:26
  40.1 10.6 %collective-permute-start.10 = (f32[24,1,768]{2,0,1:T(8,128)S(1)}, f32[24,1,768]{2,0,1:T(8,128)S(1)}, u32[]{:S(2)}, u32[]{:S(2)}) collective-permute-start(f32[24,1,768]{2,0,1:T(8,128)S(1)} %get-tuple-element.63), channel_id=1, source_target_pairs={{0,1},{1,2},{2,3},{3,4},{4,5},{5,6},{6,7},{7,8},{8,9},{9,10},{10,1... | collective-permute-start | bytes 221192 | tf_op jit(solution)/shard_map/ppermute | solution.py:26
  42.6 8.2 %collective-permute-start.11 = (f32[24,1,768]{2,0,1:T(8,128)S(1)}, f32[24,1,768]{2,0,1:T(8,128)S(1)}, u32[]{:S(2)}, u32[]{:S(2)}) collective-permute-start(f32[24,1,768]{2,0,1:T(8,128)S(1)} %get-tuple-element.65), channel_id=1, source_target_pairs={{0,1},{1,2},{2,3},{3,4},{4,5},{5,6},{6,7},{7,8},{8,9},{9,10},{10,1... | collective-permute-start | bytes 221192 | tf_op jit(solution)/shard_map/ppermute | solution.py:26
  46.8 3.9 %collective-permute-start.8 = (f32[24,1,768]{2,0,1:T(8,128)S(1)}, f32[24,1,768]{2,0,1:T(8,128)S(1)}, u32[]{:S(2)}, u32[]{:S(2)}) collective-permute-start(f32[24,1,768]{2,0,1:T(8,128)S(1)} %get-tuple-element.62), channel_id=1, source_target_pairs={{1,0},{2,1},{3,2},{4,3},{5,4},{6,5},{7,6},{8,7},{9,8},{10,9},{11,1... | collective-permute-start | bytes 221192 | tf_op jit(solution)/shard_map/ppermute | solution.py:28
  48.1 3.8 %collective-permute-start.9 = (f32[24,1,768]{2,0,1:T(8,128)S(1)}, f32[24,1,768]{2,0,1:T(8,128)S(1)}, u32[]{:S(2)}, u32[]{:S(2)}) collective-permute-start(f32[24,1,768]{2,0,1:T(8,128)S(1)} %get-tuple-element.64), channel_id=1, source_target_pairs={{1,0},{2,1},{3,2},{4,3},{5,4},{6,5},{7,6},{8,7},{9,8},{10,9},{11,1... | collective-permute-start | bytes 221192 | tf_op jit(solution)/shard_map/ppermute | solution.py:28
  55.5 6.3 %copy-start.4 = (s32[4,6]{1,0:T(4,128)S(1)}, s32[4,6]{1,0:T(4,128)}, u32[]{:S(2)}) copy-start(s32[4,6]{1,0:T(4,128)} %param.14) | copy-start | bytes 292
  55.5 39.7 %all-to-all-start = ((f32[24,32,768]{2,0,1:T(8,128)}), f32[24,32,768]{2,0,1:T(8,128)S(1)}, u32[]{:S(2)}, u32[]{:S(2)}) async-start(f32[24,32,768]{2,0,1:T(8,128)} %fusion.16), calls=%async_computation | async-start | bytes 4718592 | tf_op jit(solution)/shard_map/all_to_all | solution.py:110
  61.5 208.9 %all-reduce.8.cloned.1.call-start = ((), (), s32[]{:S(2)}) async-start(), calls=%async_computation.2 | async-start | bytes 393216 | tf_op jit(solution)/shard_map/psum | solution.py:137
  95.2 1.4 copy-start
  96.6 2.7 copy-start.1
  106.0 2.2 copy-start.2
  108.1 5.1 %copy-start.3 = (f32[4,6,32]{2,0,1:T(4,128)S(1)}, f32[4,6,32]{2,0,1:T(4,128)}, u32[]{:S(2)}) copy-start(f32[4,6,32]{2,0,1:T(4,128)} %param.15) | copy-start | bytes 9220
Sparse Core Ops, SparseCore 0:
  115.7 154.6 all-reduce.7
where the time goes:
time: 338 us; the launch traced here: 337 us
  blocking collectives  111 us (33%)
  waiting for transfers between devices  109 us (32%)
  starting transfers between devices  35.5 us (11%)
  other arithmetic  25.5 us (8%)
  matrix products  25.5 us (8%)
  local copies, waits for them, and re-layouts  15 us (4%)
  between operations  14.6 us (4%)
    psum x1, blocking collectives, body(): gram_total, rhs_total = lax.psum((gram_part, rhs_part), ('group', 'dev'))  79 us
    psum x1, waiting for transfers between devices, body(): gram_total, rhs_total = lax.psum((gram_part, rhs_part), ('group', 'dev'))  74.7 us
    all_to_all x1, waiting for transfers between devices, body(): lax.all_to_all(predict_heads, 'group', split_axis=1, concat_axis=0, tiled...  33.3 us
    all_to_all x1, blocking collectives, body(): lax.all_to_all(analysis, 'group', split_axis=0, concat_axis=1, tiled=True)  32.5 us
    ppermute x6, starting transfers between devices, padded(): lax.ppermute(tail, axis, [(i, (i + 1) % count) for i in range(ends)])  21.5 us
    mul x3, other arithmetic, soil_hydraulic_law(): hydraulic_conductance * factor  9.64 us
    all_to_all x3, local copies, waits for them, and re-layouts, body(): lax.all_to_all(predict_heads, 'group', split_axis=1, concat_axis=0, tiled...  8.33 us
    ppermute x6, starting transfers between devices, padded(): lax.ppermute(head, axis, [((i + 1) % count, i) for i in range(ends)])  7.75 us
  transfers between devices with their start and end apart: 14, of which 3 were waited for; matrix products, arithmetic and copies ran while one was open for 2% of the time, Pallas kernels for 0%

commit v1 on v0

v1 whole, which is shorter than its diff:
```python
import jax
import jax.numpy as jnp
from jax import lax
from jax.experimental import pallas as pl
from jax.experimental.pallas import tpu as pltpu
from jax.sharding import PartitionSpec as P

MEMBERS = 192
SOIL_TYPES = 8
MODEL_STEPS = 3
NEWTON_STEPS = 12
BLOCKS = 6
OBS = 32

step_duration = 0.1
gravity_head = 1.0
AXES = ("group", "dev")


def soil_values(soil_index, ks_table, alpha_table):
    soil_kinds = jnp.arange(SOIL_TYPES, dtype=jnp.int32)
    one_hot = (soil_index[None] == soil_kinds[:, None, None]).astype(jnp.float32)
    ks = jnp.sum(one_hot * ks_table[:, None, None], axis=0)
    alpha = jnp.sum(one_hot * alpha_table[:, None, None], axis=0)
    return ks, alpha


def forecast(heads, soil_index, ks_table, alpha_table):
    members, rows, columns = heads.shape
    halo = MODEL_STEPS
    count = lax.axis_size("dev")
    me = lax.axis_index("dev")
    by_row = jnp.transpose(heads, (1, 0, 2))
    soil = soil_index.astype(jnp.float32)

    def edge(lo, hi):
        return jnp.concatenate([by_row[lo:hi].reshape(halo * members, columns), soil[lo:hi]], axis=0)

    above = lax.ppermute(edge(rows - halo, rows), "dev", [(i, i + 1) for i in range(count - 1)])
    below = lax.ppermute(edge(0, halo), "dev", [(i + 1, i) for i in range(count - 1)])

    def part(block):
        cut = halo * members
        return block[:cut].reshape(halo, members, columns), block[cut:]

    above_heads, above_soil = part(above)
    below_heads, below_soil = part(below)
    h = jnp.concatenate([above_heads, by_row, below_heads], axis=0)
    kinds = jnp.concatenate([above_soil, soil, below_soil], axis=0).astype(jnp.int32)
    ks, alpha = soil_values(kinds, ks_table, alpha_table)
    row = jnp.arange(rows + 2 * halo)
    inside = ((row >= halo) | (me > 0)) & ((row < rows + halo) | (me < count - 1))
    inside = inside.astype(jnp.float32)[:, None]
    ks = (ks * inside)[:, None, :]
    alpha = alpha[:, None, :]
    inside = inside[:, :, None]
    for _ in range(MODEL_STEPS):
        factor = jnp.exp(alpha * jnp.minimum(h, 0.0))
        k = ks * factor
        capacity = 0.1 + 0.4 * alpha * factor
        flux = 0.5 * (k[1:] + k[:-1]) * (h[1:] - h[:-1])
        mid, k_mid = h[1:-1], k[1:-1]
        vertical = 0.5 * (k_mid[..., 1:] + k_mid[..., :-1]) * (mid[..., 1:] - mid[..., :-1] - gravity_head)
        border = jnp.zeros_like(mid[..., :1])
        inflow = (
            flux[1:]
            - flux[:-1]
            + jnp.concatenate([vertical, border], -1)
            - jnp.concatenate([border, vertical], -1)
        )
        h = (mid + step_duration * inflow / capacity[1:-1]) * inside[1:-1]
        ks, alpha, inside = ks[1:-1], alpha[1:-1], inside[1:-1]
    return h


def total_over_devices(x):
    count = lax.axis_size("dev")
    groups = lax.axis_size("group")
    rows = x.shape[0] // 2
    core = lax.axis_index("dev") % 2
    other = [(i, i ^ 1) for i in range(count)]
    low, high = x[:rows], x[rows:]
    mine = jnp.where(core == 0, low, high)
    x = mine + lax.ppermute(jnp.where(core == 0, high, low), "dev", other)

    def turned(size, base, k, n):
        return [(i, i + (((i // base + k) % size) - (i // base) % size) * base) for i in range(n)]

    for axis, n, base, size in (
        ("dev", count, 2, 4),
        ("group", groups, 2, groups // 2),
        ("dev", count, 8, count // 8),
        ("group", groups, 1, 2),
    ):
        arrived = [lax.ppermute(x, axis, turned(size, base, k, n)) for k in range(1, size)]
        for a in arrived:
            x = x + a
    o = lax.ppermute(x, "dev", other)
    return jnp.concatenate([jnp.where(core == 0, x, o), jnp.where(core == 0, o, x)], axis=0)


def halves(x):
    high = x.astype(jnp.bfloat16)
    return high, (x - high.astype(jnp.float32)).astype(jnp.bfloat16)


def product(a, b, dims):
    (ah, al), (bh, bl) = a, b
    dot = lambda u, v: lax.dot_general(u, v, (dims, ((), ())), preferred_element_type=jnp.float32)
    return dot(ah, bh) + (dot(ah, bl) + dot(al, bh))


NN, NT, TN = ((1,), (0,)), ((1,), (1,)), ((0,), (0,))


def gram_kernel(mask_ref, heads_ref, op_ref, values_ref, spread_ref, packed_ref, joint_ref):
    sources, share, members, columns = heads_ref.shape
    total = sources * members
    lane = lax.broadcasted_iota(jnp.int32, (OBS, 256), 1)
    for r in range(share):
        acc = heads_ref[0, r]
        for s in range(1, sources):
            acc = acc + heads_ref[s, r]
        mean = jnp.sum(acc, axis=0, keepdims=True) / total
        parts = []
        for s in range(sources):
            part = heads_ref[s, r] - mean
            spread_ref[s, r] = part
            parts.append(part)
        parts.append(jnp.broadcast_to(mean, (8, columns)))
        rows = jnp.concatenate(parts, axis=0)
        for b in range(BLOCKS):
            at = r * BLOCKS + b
            high, low = halves(rows[:, 128 * b : 128 * b + 128])
            on = (mask_ref[r, b] != 0).astype(jnp.float32)
            op_high, op_low = halves(op_ref[at] * on)
            left = jnp.concatenate(
                [
                    jnp.concatenate([op_high, op_high], 1),
                    jnp.concatenate([op_low, jnp.zeros_like(op_low)], 1),
                ],
                0,
            )
            right = jnp.concatenate([high, low], 1)
            out = lax.dot_general(left, right, (NT, ((), ())), preferred_element_type=jnp.float32)
            out = out[:OBS] + out[OBS:]
            out = jnp.pad(out, ((0, 0), (0, 256 - out.shape[1])))
            innovation = values_ref[:, at : at + 1] * on - out
            joint = jnp.where(lane < total, out, jnp.where(lane == total, innovation, 0.0))
            joint_ref[OBS * at : OBS * at + OBS, :] = joint
    both = halves(joint_ref[...])
    gram = product(both, both, TN)
    side = lax.broadcasted_iota(jnp.int32, (64, 128), 1)
    packed_ref[0:64] = jnp.where(side < 64, gram[0:64, :128], gram[64:128, :128])
    packed_ref[64:128] = jnp.where(side < 64, gram[64:128, :128], pltpu.roll(gram[128:192, 128:], 64, 1))
    packed_ref[128:192] = gram[128:192, :128]
    packed_ref[192:200] = gram[192:200, :128]
    packed_ref[200:208] = gram[192:200, 128:]


def mean_and_gram(heads, op, mask, values):
    sources, share, members, columns = heads.shape
    anywhere = pl.BlockSpec(memory_space=pltpu.VMEM)
    return pl.pallas_call(
        gram_kernel,
        out_shape=(
            jax.ShapeDtypeStruct(heads.shape, jnp.float32),
            jax.ShapeDtypeStruct((208, 128), jnp.float32),
        ),
        in_specs=[pl.BlockSpec(memory_space=pltpu.SMEM), anywhere, anywhere, anywhere],
        out_specs=(anywhere, anywhere),
        scratch_shapes=[pltpu.VMEM((share * BLOCKS * OBS, 256), jnp.float32)],
        compiler_params=pltpu.CompilerParams(vmem_limit_bytes=40 * 2**20),
        name="gram",
    )(mask, heads, op, values)


def newton_kernel(packed_ref, out_ref, gram_ref):
    order = MEMBERS
    side = lax.broadcasted_iota(jnp.int32, (64, 128), 1)
    p0, p1, p2 = packed_ref[0:64], packed_ref[64:128], packed_ref[128:192]
    below = jnp.where(side < 64, p1, p0)
    turned = jnp.concatenate([p0, below], 0).T
    gram_ref[0:64, 0:128] = jnp.where(side < 64, p0, turned[0:64])
    gram_ref[64:128, 0:128] = below
    gram_ref[128:192, 0:128] = p2
    gram_ref[0:128, 128:192] = p2.T
    gram_ref[128:192, 128:192] = pltpu.roll(p1, 64, 1)[:, :64]
    eye = (
        lax.broadcasted_iota(jnp.int32, (order, order), 0)
        == lax.broadcasted_iota(jnp.int32, (order, order), 1)
    ).astype(jnp.float32)
    gram = gram_ref[...] + (MEMBERS - 1.0) * eye
    rhs = jnp.concatenate([packed_ref[192:200], packed_ref[200:208, :64]], 1)
    norm = jnp.sum(jnp.abs(gram), keepdims=True)
    inverse_norm = 1.0 / norm
    iterate = gram * inverse_norm
    middle = 1.5 * eye - 0.5 * iterate
    iterate = product(halves(iterate), halves(middle), NN)
    inverse = middle
    for step in range(1, NEWTON_STEPS):
        left = halves(inverse)
        middle = 1.5 * eye - 0.5 * product(left, halves(iterate), NN)
        right = halves(middle)
        if step < NEWTON_STEPS - 1:
            iterate = product(halves(iterate), right, NN)
        inverse = product(left, right, NN)
    final = halves(inverse)
    shift = product(halves(product(halves(rhs), final, NN)), final, NN) * inverse_norm
    out_ref[...] = jnp.sqrt((MEMBERS - 1.0) * inverse_norm) * inverse + shift[0:1]


def newton_weights(packed):
    return pl.pallas_call(
        newton_kernel,
        out_shape=jax.ShapeDtypeStruct((MEMBERS, MEMBERS), jnp.float32),
        in_specs=[pl.BlockSpec(memory_space=pltpu.VMEM)],
        out_specs=pl.BlockSpec(memory_space=pltpu.VMEM),
        scratch_shapes=[pltpu.VMEM((MEMBERS, MEMBERS), jnp.float32)],
        compiler_params=pltpu.CompilerParams(vmem_limit_bytes=40 * 2**20),
        name="newton",
    )(packed)


def mix_kernel(weights_ref, spread_ref, out_ref):
    sources, share, members, columns = spread_ref.shape
    weights = halves(weights_ref[...])
    for r in range(share):
        for c in range(0, columns, 256):
            s = jnp.concatenate([spread_ref[g, r, :, c : c + 256] for g in range(sources)], 0)
            mixed = product(weights, halves(s), NN)
            for g in range(sources):
                out_ref[g, r, :, c : c + 256] = mixed[members * g : members * g + members]


def mix(weights, spread):
    anywhere = pl.BlockSpec(memory_space=pltpu.VMEM)
    return pl.pallas_call(
        mix_kernel,
        out_shape=jax.ShapeDtypeStruct(spread.shape, jnp.float32),
        in_specs=[anywhere, anywhere],
        out_specs=anywhere,
        compiler_params=pltpu.CompilerParams(vmem_limit_bytes=40 * 2**20),
        name="mix",
    )(weights, spread)


def body(member_pressure_heads, soil_index, ks_table, alpha_table, obs_op, obs_mask, obs_values):
    predicted = forecast(member_pressure_heads, soil_index, ks_table, alpha_table)
    rows, members, columns = predicted.shape
    groups = lax.axis_size("group")
    share = rows // groups
    heads = lax.all_to_all(predicted.reshape(groups, share, members, columns), "group", 0, 0, tiled=True)
    op = obs_op.reshape(share * BLOCKS, OBS, 128)
    values = obs_values.reshape(share * BLOCKS, OBS).T
    spread, part = mean_and_gram(heads, op, obs_mask, values)
    mixed = mix(newton_weights(total_over_devices(part)), spread)
    back = lax.all_to_all(mixed, "group", 0, 0, tiled=True)
    return jnp.transpose(back.reshape(rows, members, columns), (1, 0, 2))


def solution(mesh):
    placed = (
        P("group", "dev", None),
        P("dev", None),
        P(),
        P(),
        P(("dev", "group"), None, None, None),
        P(("dev", "group"), None),
        P(("dev", "group"), None, None),
    )
    return jax.shard_map(
        body, mesh=mesh, in_specs=placed, out_specs=P("group", "dev", None), check_vma=False
    )
```

time: 338 us -> 149 us (0.44)
  blocking collectives: 111 us -> 34.2 us
  waiting for transfers between devices: 109 us -> 48.6 us
  matrix products: 25.5 us -> 0 us
  between operations: 14.6 us -> 0.36 us
  Pallas kernels: 0 us -> 10.3 us
  local copies, waits for them, and re-layouts: 15 us -> 7.02 us
  other arithmetic: 25.5 us -> 17.8 us
  starting transfers between devices: 35.5 us -> 29.3 us
    psum x1 -> x0, blocking collectives: 79 us -> none  [body(): gram_total, rhs_total = lax.psum((gram_part, rhs_part), ('group', 'dev'))]
    psum x1 -> x0, waiting for transfers between devices: 74.7 us -> none  [body(): gram_total, rhs_total = lax.psum((gram_part, rhs_part), ('group', 'dev'))]
    dot_general x43 -> x0, matrix products: 25.5 us -> none  [the longest x12 6.96 us: one_turn(): jnp.dot(iterate, middle, precision=highest, preferred_element_type=jnp.fl...]
    ppermute x12, waiting for transfers between devices: 1.2 us -> 16 us  [the longest x8 10.3 us: total_over_devices(): lax.ppermute(x, axis, turned(size, base, k, n))]
    all_to_all x5 -> x0, local copies, waits for them, and re-layouts: 10.8 us -> none  [the longest x3 8.33 us: body(): lax.all_to_all(predict_heads, 'group', split_axis=1, concat_axis=0, tiled...]
    pallas_call x0 -> x3, Pallas kernels: none -> 10.3 us  [the longest x1 7.03 us: newton_weights(): pl.pallas_call(newton_kernel, out_shape=jax.ShapeDtypeStruct((MEMBERS, ME...]
    ppermute x12, starting transfers between devices: 29.2 us -> 23.4 us  [the longest x8 18.7 us: total_over_devices(): lax.ppermute(x, axis, turned(size, base, k, n))]
    add x1 -> x5, other arithmetic: 3.53 us -> 0.07 us  [the longest x4 0.06 us: total_over_devices(): x = x + a]
  transfers between devices with their start and end apart: 14 -> 13, of which waited for: 3 -> 11; matrix products, arithmetic and copies ran while one was open for 2% -> 0% of each run, Pallas kernels for 0% -> 0%
where the time goes in v1:
time: 149 us; the launch traced here: 148 us
  waiting for transfers between devices  48.6 us (33%)
  blocking collectives  34.2 us (23%)
  starting transfers between devices  29.3 us (20%)
  other arithmetic  17.8 us (12%)
  Pallas kernels  10.3 us (7%)
  local copies, waits for them, and re-layouts  7.02 us (5%)
    all_to_all x1, blocking collectives, body(): back = lax.all_to_all(mixed, 'group', 0, 0, tiled=True)  34.2 us
    all_to_all x1, waiting for transfers between devices, body(): lax.all_to_all(predicted.reshape(groups, share, members, columns), 'group...  32.6 us
    ppermute x8, starting transfers between devices, total_over_devices(): lax.ppermute(x, axis, turned(size, base, k, n))  18.7 us
    ppermute x8, waiting for transfers between devices, total_over_devices(): lax.ppermute(x, axis, turned(size, base, k, n))  10.3 us
    pallas_call x1, Pallas kernels, newton_weights(): pl.pallas_call(newton_kernel, out_shape=jax.ShapeDtypeStruct((MEMBERS, ME...  7.03 us
    mul x3, other arithmetic, forecast(): k = ks * factor  6.76 us
    all_to_all x1, starting transfers between devices, body(): lax.all_to_all(predicted.reshape(groups, share, members, columns), 'group...  5.96 us
    mul x3, other arithmetic, forecast(): 0.5 * (k_mid[..., 1:] + k_mid[..., :-1])  5.22 us
  transfers between devices with their start and end apart: 13, of which 11 were waited for; matrix products, arithmetic and copies ran while one was open for 0% of the time, Pallas kernels for 0%

profile of v1, /device:TPU:0, one launch (start us, length us, event | category | flops | bytes accessed | tf_op | source)
XLA Modules:
  0.0 147.5 jit_solution(10484664021893893357)
XLA Ops:
  5.6 3.5 %collective-permute-done.1 = f32[75,768]{1,0:T(8,128)S(1)} collective-permute-done((f32[75,768]{1,0:T(8,128)S(1)}, f32[75,768]{1,0:T(8,128)S(1)}, u32[]{:S(2)}, u32[]{:S(2)}) %collective-permute-start.1) | collective-permute-done | bytes 230432 | tf_op jit(solution)/shard_map/ppermute | solution.py:40
  11.7 1.9 %fusion.19 = f32[36,24,767]{2,0,1:T(8,128)S(1)} fusion(f32[38,24,768]{2,0,1:T(8,128)S(1)} %get-tuple-element.19, f32[38,24,768]{2,0,1:T(8,128)S(1)} %get-tuple-element.17), kind=kLoop, calls=%fused_computation.29 | loop fusion | flops 3313440 | bytes 13253760 | tf_op jit(solution)/shard_map/mul | solution.py:63
  13.6 3.0 %broadcast_multiply_fusion.1 = (f32[36,24,768]{2,0,1:T(8,128)S(1)}, f32[36,24,768]{2,0,1:T(8,128)S(1)}, f32[36,24,768]{2,0,1:T(8,128)S(1)}) fusion(f32[36,768]{1,0:T(8,128)S(1)} %slice.262, f32[36,768]{1,0:T(8,128)S(1)} %get-tuple-element.25, f32[36]{0:T(128)S(1)} %slice.207, f32[38,24,768]{2,0,1:T(8,128)S(1)} %get-tuple-element.18, ...), kind=kLoop, calls=%fused_computation.60 | loop fusion | flops 7962624 | bytes 21562128 | tf_op jit(solution)/shard_map/mul | solution.py:59
  17.4 1.9 %fusion.7 = f32[34,24,767]{2,0,1:T(8,128)S(1)} fusion(f32[36,24,768]{2,0,1:T(8,128)S(1)} %get-tuple-element.16, f32[36,24,768]{2,0,1:T(8,128)S(1)} %get-tuple-element.14), kind=kLoop, calls=%fused_computation.11 | loop fusion | flops 3129360 | bytes 12517440 | tf_op jit(solution)/shard_map/mul | solution.py:63
  19.4 2.9 %broadcast_multiply_fusion = (f32[34,24,768]{2,0,1:T(8,128)S(1)}, f32[34,24,768]{2,0,1:T(8,128)S(1)}, f32[34,24,768]{2,0,1:T(8,128)S(1)}) fusion(f32[34,768]{1,0:T(8,128)S(1)} %slice.277, f32[34,768]{1,0:T(8,128)S(1)} %get-tuple-element.23, f32[34]{0:T(128)S(1)} %slice.222, f32[36,24,768]{2,0,1:T(8,128)S(1)} %get-tuple-element.15, f32[34,768]{1,0:T(8,128)S(1)} %slice.274, ...), kind=kLoop, calls=%fused_computation.59 | loop fusion | flops 7520256 | bytes 20364232 | tf_op jit(solution)/shard_map/mul | solution.py:59
  22.2 1.5 %fusion.31 = f32[32,24,767]{2,0,1:T(8,128)S(1)} fusion(f32[34,24,768]{2,0,1:T(8,128)S(1)} %get-tuple-element.13, f32[34,24,768]{2,0,1:T(8,128)S(1)} %get-tuple-element.11), kind=kLoop, calls=%fused_computation.51 | loop fusion | flops 2945280 | bytes 11781120 | tf_op jit(solution)/shard_map/mul | solution.py:63
  24.5 1.5 %fusion.29 = f32[32,24,768]{2,0,1:T(8,128)S(1)} fusion(f32[34,24,768]{2,0,1:T(8,128)S(1)} %get-tuple-element.12, f32[33,24,768]{2,0,1:T(8,128)S(1)} %fusion, f32[34,24,768]{2,0,1:T(8,128)S(1)} %get-tuple-element.13, f32[32,24,767]{2,0,1:T(8,128)S(1)} %fusion.31, f32[32,768]{1,0:T(8,128)S(1)} %slice.289, f32[32]{0:T(128)S(1)} %slice.237), kind=kLoop, calls=%fused_computation.48 | loop fusion | flops 5308416 | bytes 14251136 | tf_op jit(solution)/shard_map/mul | solution.py:71
  26.1 2.8 %copy.27 = f32[32,24,768]{2,1,0:T(8,128)} copy(f32[32,24,768]{2,0,1:T(8,128)S(1)} %fusion.29) | data formatting | bytes 4718592 | tf_op jit(solution)/shard_map/mul | solution.py:71
  28.9 6.0 %all-to-all-start = ((f32[8,4,24,768]{3,2,1,0:T(8,128)}), f32[8,4,24,768]{3,2,1,0:T(8,128)S(1)}, u32[]{:S(2)}, u32[]{:S(2)}) async-start(f32[8,4,24,768]{3,2,1,0:T(8,128)} %bitcast.14), calls=%async_computation | async-start | bytes 4718592 | tf_op jit(solution)/shard_map/all_to_all | solution.py:253
  34.9 32.6 %all-to-all-done.heads_ref = f32[8,4,24,768]{3,2,1,0:T(8,128)S(1)} async-done(((f32[8,4,24,768]{3,2,1,0:T(8,128)}), f32[8,4,24,768]{3,2,1,0:T(8,128)S(1)}, u32[]{:S(2)}, u32[]{:S(2)}) %all-to-all-start) | async-done | bytes 2359328 | tf_op jit(solution)/shard_map/all_to_all | solution.py:253
  67.6 2.2 %gram.1 = (f32[8,4,24,768]{3,2,1,0:T(8,128)S(1)}, f32[208,128]{1,0:T(8,128)S(1)}) custom-call(s32[4,6]{1,0:T(4,128)S(1)} %copy-done.1, f32[8,4,24,768]{3,2,1,0:T(8,128)S(1)} %all-to-all-done.heads_ref, f32[24,32,128]{2,1,0:T(8,128)S(1)} %bitcast.12, f32[32,24]{1,0:T(8,128)S(1)} %bitcast.13), custom_call_target="tpu_custom_call" | custom-call | tf_op jit(solution)/shard_map/gram/pallas_call | solution.py:164
  69.7 2.0 %collective-permute-start.2 = (f32[104,128]{1,0:T(8,128)S(1)}, f32[104,128]{1,0:T(8,128)S(1)}, u32[]{:S(2)}, u32[]{:S(2)}) collective-permute-start(f32[104,128]{1,0:T(8,128)S(1)} %slice_select_fusion), channel_id=1, source_target_pairs={{0,1},{1,0},{2,3},{3,2},{4,5},{5,4},{6,7},{7,6},{8,9},{9,8},{10,11... | collective-permute-start | bytes 159752 | tf_op jit(solution)/shard_map/ppermute | solution.py:84
  72.7 5.7 %collective-permute-start.3 = (f32[104,128]{1,0:T(8,128)S(1)}, f32[104,128]{1,0:T(8,128)S(1)}, u32[]{:S(2)}, u32[]{:S(2)}) collective-permute-start(f32[104,128]{1,0:T(8,128)S(1)} %select_add_fusion), channel_id=1, source_target_pairs={{0,2},{1,3},{2,4},{3,5},{4,6},{5,7},{6,0},{7,1},{8,10},{9,11},{10,... | collective-permute-start | bytes 159752 | tf_op jit(solution)/shard_map/ppermute | solution.py:95
  78.3 1.9 %collective-permute-start.4 = (f32[104,128]{1,0:T(8,128)S(1)}, f32[104,128]{1,0:T(8,128)S(1)}, u32[]{:S(2)}, u32[]{:S(2)}) collective-permute-start(f32[104,128]{1,0:T(8,128)S(1)} %select_add_fusion), channel_id=1, source_target_pairs={{0,4},{1,5},{2,6},{3,7},{4,0},{5,1},{6,2},{7,3},{8,12},{9,13},{10,... | collective-permute-start | bytes 159752 | tf_op jit(solution)/shard_map/ppermute | solution.py:95
  80.2 2.5 %collective-permute-start.5 = (f32[104,128]{1,0:T(8,128)S(1)}, f32[104,128]{1,0:T(8,128)S(1)}, u32[]{:S(2)}, u32[]{:S(2)}) collective-permute-start(f32[104,128]{1,0:T(8,128)S(1)} %select_add_fusion), channel_id=1, source_target_pairs={{0,6},{1,7},{2,0},{3,1},{4,2},{5,3},{6,4},{7,5},{8,14},{9,15},{10,... | collective-permute-start | bytes 159752 | tf_op jit(solution)/shard_map/ppermute | solution.py:95
  84.9 2.7 %collective-permute-start.7 = (f32[104,128]{1,0:T(8,128)S(1)}, f32[104,128]{1,0:T(8,128)S(1)}, u32[]{:S(2)}, u32[]{:S(2)}) collective-permute-start(f32[104,128]{1,0:T(8,128)S(1)} %add_add_fusion.1), channel_id=1, source_target_pairs={{0,64},{16,80},{32,96},{48,112},{64,0},{80,16},{96,32},{112,48},{1... | collective-permute-start | bytes 159752 | tf_op jit(solution)/shard_map/ppermute | solution.py:95
  87.9 2.1 %collective-permute-done.6 = f32[104,128]{1,0:T(8,128)S(1)} collective-permute-done((f32[104,128]{1,0:T(8,128)S(1)}, f32[104,128]{1,0:T(8,128)S(1)}, u32[]{:S(2)}, u32[]{:S(2)}) %collective-permute-start.6) | collective-permute-done | bytes 53280 | tf_op jit(solution)/shard_map/ppermute | solution.py:95
  91.7 3.7 %collective-permute-start.9 = (f32[104,128]{1,0:T(8,128)S(1)}, f32[104,128]{1,0:T(8,128)S(1)}, u32[]{:S(2)}, u32[]{:S(2)}) collective-permute-start(f32[104,128]{1,0:T(8,128)S(1)} %add_add_fusion), channel_id=1, source_target_pairs={{0,8},{1,9},{2,10},{3,11},{4,12},{5,13},{6,14},{7,15},{8,0},{9,1},... | collective-permute-start | bytes 159752 | tf_op jit(solution)/shard_map/ppermute | solution.py:95
  95.4 2.1 %collective-permute-done.9 = f32[104,128]{1,0:T(8,128)S(1)} collective-permute-done((f32[104,128]{1,0:T(8,128)S(1)}, f32[104,128]{1,0:T(8,128)S(1)}, u32[]{:S(2)}, u32[]{:S(2)}) %collective-permute-start.9) | collective-permute-done | bytes 53280 | tf_op jit(solution)/shard_map/ppermute | solution.py:95
  97.5 1.6 %collective-permute-start.10 = (f32[104,128]{1,0:T(8,128)S(1)}, f32[104,128]{1,0:T(8,128)S(1)}, u32[]{:S(2)}, u32[]{:S(2)}) collective-permute-start(f32[104,128]{1,0:T(8,128)S(1)} %add.118), channel_id=1, source_target_pairs={{0,16},{16,0},{32,48},{48,32},{64,80},{80,64},{96,112},{112,96},{1... | collective-permute-start | bytes 159752 | tf_op jit(solution)/shard_map/ppermute | solution.py:95
  99.1 2.6 %collective-permute-done.10 = f32[104,128]{1,0:T(8,128)S(1)} collective-permute-done((f32[104,128]{1,0:T(8,128)S(1)}, f32[104,128]{1,0:T(8,128)S(1)}, u32[]{:S(2)}, u32[]{:S(2)}) %collective-permute-start.10) | collective-permute-done | bytes 53280 | tf_op jit(solution)/shard_map/ppermute | solution.py:95
  103.1 7.0 %newton.1.weights_ref = f32[192,192]{1,0:T(8,128)S(1)} custom-call(f32[208,128]{1,0:T(8,128)S(1)} %pad_maximum_fusion.3.packed_ref), custom_call_target="tpu_custom_call" | custom-call | tf_op jit(solution)/shard_map/newton/pallas_call | solution.py:214
  111.2 34.2 %all_to_all.10 = f32[8,4,24,768]{3,2,1,0:T(8,128)S(1)} all-to-all(f32[8,4,24,768]{3,2,1,0:T(8,128)S(1)} %mix.1), channel_id=1, replica_groups=mesh['group'=8,'dev'=16] {'group'}, dimensions={0} | all-to-all | bytes 4718592 | tf_op jit(solution)/shard_map/all_to_all | solution.py:258
  145.4 2.1 %copy.32 = f32[32,24,768]{2,0,1:T(8,128)} copy(f32[32,24,768]{2,1,0:T(8,128)S(1)} %bitcast.15) | data formatting | bytes 4718592 | tf_op jit(solution)/shard_map/reshape | solution.py:259
  (68 shorter events, 17.2 us)
Async XLA Ops:
  0.0 9.3 %copy-start.5 = (f32[8]{0:T(128)S(1)}, f32[8]{0:T(128)}, u32[]{:S(2)}) copy-start(f32[8]{0:T(128)} %param.10) | copy-start | bytes 100
  0.0 9.3 %copy-start.4 = (f32[8]{0:T(128)S(1)}, f32[8]{0:T(128)}, u32[]{:S(2)}) copy-start(f32[8]{0:T(128)} %param.9) | copy-start | bytes 100
  1.4 8.7 %copy-start.2 = (f32[24,32,768]{2,1,0:T(8,128)S(1)}, f32[24,32,768]{2,1,0:T(8,128)}, u32[]{:S(2)}) copy-start(f32[24,32,768]{2,1,0:T(8,128)} %param.7) | copy-start | bytes 7077892
  2.5 2.9 %collective-permute-start = (f32[75,768]{1,0:T(8,128)S(1)}, f32[75,768]{1,0:T(8,128)S(1)}, u32[]{:S(2)}, u32[]{:S(2)}) collective-permute-start(f32[75,768]{1,0:T(8,128)S(1)} %pad_maximum_fusion.1), channel_id=1, source_target_pairs={{0,1},{1,2},{2,3},{3,4},{4,5},{5,6},{6,7},{7,8},{8,9},{9,10},{10,1... | collective-permute-start | bytes 691208 | tf_op jit(solution)/shard_map/ppermute | solution.py:39
  3.9 5.2 %collective-permute-start.1 = (f32[75,768]{1,0:T(8,128)S(1)}, f32[75,768]{1,0:T(8,128)S(1)}, u32[]{:S(2)}, u32[]{:S(2)}) collective-permute-start(f32[75,768]{1,0:T(8,128)S(1)} %pad_maximum_fusion.2), channel_id=1, source_target_pairs={{1,0},{2,1},{3,2},{4,3},{5,4},{6,5},{7,6},{8,7},{9,8},{10,9},{11,1... | collective-permute-start | bytes 691208 | tf_op jit(solution)/shard_map/ppermute | solution.py:40
  28.8 6.0 %copy-start.3 = (f32[4,6,32]{2,0,1:T(4,128)S(1)}, f32[4,6,32]{2,0,1:T(4,128)}, u32[]{:S(2)}) copy-start(f32[4,6,32]{2,0,1:T(4,128)} %param.13) | copy-start | bytes 9220
  28.8 38.7 %copy-start = (f32[4,6,32,128]{3,2,1,0:T(8,128)S(1)}, f32[4,6,32,128]{3,2,1,0:T(8,128)}, u32[]{:S(2)}) copy-start(f32[4,6,32,128]{3,2,1,0:T(8,128)} %param.11) | copy-start | bytes 1179652
  28.8 38.7 %copy-start.1 = (s32[4,6]{1,0:T(4,128)S(1)}, s32[4,6]{1,0:T(4,128)}, u32[]{:S(2)}) copy-start(s32[4,6]{1,0:T(4,128)} %mask_ref.1) | copy-start | bytes 292
  28.9 38.7 %all-to-all-start = ((f32[8,4,24,768]{3,2,1,0:T(8,128)}), f32[8,4,24,768]{3,2,1,0:T(8,128)S(1)}, u32[]{:S(2)}, u32[]{:S(2)}) async-start(f32[8,4,24,768]{3,2,1,0:T(8,128)} %bitcast.14), calls=%async_computation | async-start | bytes 4718592 | tf_op jit(solution)/shard_map/all_to_all | solution.py:253
  69.7 2.9 %collective-permute-start.2 = (f32[104,128]{1,0:T(8,128)S(1)}, f32[104,128]{1,0:T(8,128)S(1)}, u32[]{:S(2)}, u32[]{:S(2)}) collective-permute-start(f32[104,128]{1,0:T(8,128)S(1)} %slice_select_fusion), channel_id=1, source_target_pairs={{0,1},{1,0},{2,3},{3,2},{4,5},{5,4},{6,7},{7,6},{8,9},{9,8},{10,11... | collective-permute-start | bytes 159752 | tf_op jit(solution)/shard_map/ppermute | solution.py:84
  72.7 10.1 %collective-permute-start.3 = (f32[104,128]{1,0:T(8,128)S(1)}, f32[104,128]{1,0:T(8,128)S(1)}, u32[]{:S(2)}, u32[]{:S(2)}) collective-permute-start(f32[104,128]{1,0:T(8,128)S(1)} %select_add_fusion), channel_id=1, source_target_pairs={{0,2},{1,3},{2,4},{3,5},{4,6},{5,7},{6,0},{7,1},{8,10},{9,11},{10,... | collective-permute-start | bytes 159752 | tf_op jit(solution)/shard_map/ppermute | solution.py:95
  78.3 5.6 %collective-permute-start.4 = (f32[104,128]{1,0:T(8,128)S(1)}, f32[104,128]{1,0:T(8,128)S(1)}, u32[]{:S(2)}, u32[]{:S(2)}) collective-permute-start(f32[104,128]{1,0:T(8,128)S(1)} %select_add_fusion), channel_id=1, source_target_pairs={{0,4},{1,5},{2,6},{3,7},{4,0},{5,1},{6,2},{7,3},{8,12},{9,13},{10,... | collective-permute-start | bytes 159752 | tf_op jit(solution)/shard_map/ppermute | solution.py:95
  80.2 4.3 %collective-permute-start.5 = (f32[104,128]{1,0:T(8,128)S(1)}, f32[104,128]{1,0:T(8,128)S(1)}, u32[]{:S(2)}, u32[]{:S(2)}) collective-permute-start(f32[104,128]{1,0:T(8,128)S(1)} %select_add_fusion), channel_id=1, source_target_pairs={{0,6},{1,7},{2,0},{3,1},{4,2},{5,3},{6,4},{7,5},{8,14},{9,15},{10,... | collective-permute-start | bytes 159752 | tf_op jit(solution)/shard_map/ppermute | solution.py:95
  84.6 5.4 %collective-permute-start.6 = (f32[104,128]{1,0:T(8,128)S(1)}, f32[104,128]{1,0:T(8,128)S(1)}, u32[]{:S(2)}, u32[]{:S(2)}) collective-permute-start(f32[104,128]{1,0:T(8,128)S(1)} %add_add_fusion.1), channel_id=1, source_target_pairs={{0,32},{16,48},{32,64},{48,80},{64,96},{80,112},{96,0},{112,16},{1... | collective-permute-start | bytes 159752 | tf_op jit(solution)/shard_map/ppermute | solution.py:95
  84.9 5.7 %collective-permute-start.7 = (f32[104,128]{1,0:T(8,128)S(1)}, f32[104,128]{1,0:T(8,128)S(1)}, u32[]{:S(2)}, u32[]{:S(2)}) collective-permute-start(f32[104,128]{1,0:T(8,128)S(1)} %add_add_fusion.1), channel_id=1, source_target_pairs={{0,64},{16,80},{32,96},{48,112},{64,0},{80,16},{96,32},{112,48},{1... | collective-permute-start | bytes 159752 | tf_op jit(solution)/shard_map/ppermute | solution.py:95
  87.6 4.1 %collective-permute-start.8 = (f32[104,128]{1,0:T(8,128)S(1)}, f32[104,128]{1,0:T(8,128)S(1)}, u32[]{:S(2)}, u32[]{:S(2)}) collective-permute-start(f32[104,128]{1,0:T(8,128)S(1)} %add_add_fusion.1), channel_id=1, source_target_pairs={{0,96},{16,112},{32,0},{48,16},{64,32},{80,48},{96,64},{112,80},{1... | collective-permute-start | bytes 159752 | tf_op jit(solution)/shard_map/ppermute | solution.py:95
  91.7 5.8 %collective-permute-start.9 = (f32[104,128]{1,0:T(8,128)S(1)}, f32[104,128]{1,0:T(8,128)S(1)}, u32[]{:S(2)}, u32[]{:S(2)}) collective-permute-start(f32[104,128]{1,0:T(8,128)S(1)} %add_add_fusion), channel_id=1, source_target_pairs={{0,8},{1,9},{2,10},{3,11},{4,12},{5,13},{6,14},{7,15},{8,0},{9,1},... | collective-permute-start | bytes 159752 | tf_op jit(solution)/shard_map/ppermute | solution.py:95
  97.5 4.2 %collective-permute-start.10 = (f32[104,128]{1,0:T(8,128)S(1)}, f32[104,128]{1,0:T(8,128)S(1)}, u32[]{:S(2)}, u32[]{:S(2)}) collective-permute-start(f32[104,128]{1,0:T(8,128)S(1)} %add.118), channel_id=1, source_target_pairs={{0,16},{16,0},{32,48},{48,32},{64,80},{80,64},{96,112},{112,96},{1... | collective-permute-start | bytes 159752 | tf_op jit(solution)/shard_map/ppermute | solution.py:95
  101.7 1.3 collective-permute-start.11

commit v2 on v1

--- a/solution.py
+++ b/solution.py
@@ -12,65 +12,244 @@
 BLOCKS = 6
 OBS = 32
 
-step_duration = 0.1
+HALO = MODEL_STEPS
+LN2 = 0.6931471805599453
+UNROLL = 4
+EDGE_MIB = 60
 gravity_head = 1.0
 AXES = ("group", "dev")
 
 
-def soil_values(soil_index, ks_table, alpha_table):
-    soil_kinds = jnp.arange(SOIL_TYPES, dtype=jnp.int32)
-    one_hot = (soil_index[None] == soil_kinds[:, None, None]).astype(jnp.float32)
-    ks = jnp.sum(one_hot * ks_table[:, None, None], axis=0)
-    alpha = jnp.sum(one_hot * alpha_table[:, None, None], axis=0)
+def edges_kernel(ks_table, alpha_table, first_ref, last_ref, soil_ref, top_ref, bottom_ref, ks_ref, alpha_ref):
+    members, span, columns = first_ref.shape
+    rows = soil_ref.shape[0]
+    ks, alpha = soil_tables(soil_ref[...], ks_table, alpha_table)
+    ks_ref[...] = ks
+    alpha_ref[...] = alpha
+    flag = jnp.ones((8 - 2 * HALO, columns), jnp.float32)
+    for j in range(HALO):
+        top_ref[members * j : members * j + members] = first_ref[:, j, :]
+        bottom_ref[members * j : members * j + members] = last_ref[:, span - HALO + j, :]
+    top_ref[HALO * members :] = jnp.concatenate([ks[:HALO], alpha[:HALO], flag], 0)
+    bottom_ref[HALO * members :] = jnp.concatenate([ks[rows - HALO :], alpha[rows - HALO :], flag], 0)
+
+
+def law(h, ks, alpha, slope):
+    factor = jnp.exp2(alpha * jnp.minimum(h, 0.0))
+    return ks * factor, 1.0 / (1.0 + slope * factor)
+
+
+def moved(h_ref, k_ref, gain_ref, low, count, members, inner):
+    size = members * count
+    around = slice(members * (low - 1), members * (low + count + 1))
+    h_all, k_all = h_ref[around], k_ref[around]
+    columns = h_all.shape[1]
+    flux = (k_all[members:] + k_all[:-members]) * (h_all[members:] - h_all[:-members])
+    h, k = h_all[members : members + size], k_all[members : members + size]
+    face = (k + pltpu.roll(k, columns - 1, 1)) * ((pltpu.roll(h, columns - 1, 1) - gravity_head) - h)
+    face = jnp.concatenate([face[:, : columns - 128], face[:, columns - 128 :] * inner], 1)
+    gain = gain_ref[members * low : members * (low + count)]
+    return h + gain * ((flux[members:] - flux[:size]) + (face - pltpu.roll(face, 1, 1)))
+
+
+def soil_tables(kinds, ks_ref, alpha_ref):
+    ks = jnp.zeros(kinds.shape, jnp.float32)
+    alpha = jnp.zeros(kinds.shape, jnp.float32)
+    for t in range(SOIL_TYPES):
+        ks = jnp.where(kinds == t, 0.5 * ks_ref[t], ks)
+        alpha = jnp.where(kinds == t, alpha_ref[t] / LN2, alpha)
     return ks, alpha
+
+
+def rule(h, ks_ref, alpha_ref, low, count, members):
+    def wide(rows):
+        return jnp.concatenate([jnp.broadcast_to(x, (members, x.shape[1])) for x in rows], 0)
+
+    alpha = [alpha_ref[r : r + 1] for r in range(low, low + count)]
+    return law(
+        h,
+        wide([ks_ref[r : r + 1] for r in range(low, low + count)]),
+        wide(alpha),
+        wide([(4.0 * LN2) * x for x in alpha]),
+    )
+
+
+def inner_mask():
+    return (lax.broadcasted_iota(jnp.int32, (1, 128), 1) < 127).astype(jnp.float32)
+
+
+def interior_kernel(heads_ref, ks_ref, alpha_ref, out_ref, saved_ref, given, h0, h1, k0, k1, g0, g1, sems, in_sems, save_sems):
+    members, rows, columns = given.shape
+    tile = 8
+    loads = [
+        pltpu.make_async_copy(heads_ref.at[:, t : t + tile], given.at[:, t : t + tile], in_sems.at[t // tile])
+        for t in range(0, rows, tile)
+    ]
+    for load in loads:
+        load.start()
+    inner = inner_mask()
+    at = lambda r, n: slice(members * r, members * (r + n))
+    for r in range(0, rows, 2):
+        if r % tile == 0:
+            loads[r // tile].wait()
+        h = jnp.concatenate([given[:, r, :], given[:, r + 1, :]], 0)
+        h0[at(r, 2)] = h
+        k0[at(r, 2)], g0[at(r, 2)] = rule(h, ks_ref, alpha_ref, r, 2, members)
+    now, later = (h0, k0, g0), (h1, k1, g1)
+    copies = []
+
+    def keep(ref, low, count, to):
+        copies.append(pltpu.make_async_copy(ref.at[at(low, count)], saved_ref.at[at(to, count)], save_sems.at[len(copies)]))
+        copies[-1].start()
+
+    for step in range(1, MODEL_STEPS + 1):
+        for low in range(step, rows - step, UNROLL):
+            count = min(UNROLL, rows - step - low)
+            h = moved(*now, low, count, members, inner)
+            later[0][at(low, count)] = h
+            if step < MODEL_STEPS:
+                later[1][at(low, count)], later[2][at(low, count)] = rule(h, ks_ref, alpha_ref, low, count, members)
+            else:
+                for r in range(low, low + count):
+                    copies.append(pltpu.make_async_copy(later[0].at[at(r, 1)], out_ref.at[r], sems.at[r]))
+                    copies[-1].start()
+        if step == 2:
+            keep(h0, 0, 4, 0)
+            keep(h0, rows - 4, 4, 4)
+            keep(h1, 1, 2, 8)
+            keep(h1, rows - 3, 2, 10)
+        now, later = later, now
+    for copy in copies:
+        copy.wait()
+
+
+def edge_kernel(above_ref, below_ref, saved_ref, own_ks, own_alpha, given_ref, out_ref, *scratch):
+    del given_ref
+    *states, ks_ref, alpha_ref, sems, in_sems = scratch
+    rows, columns = own_ks.shape
+    members = saved_ref.shape[0] // 12
+    inner = inner_mask()
+    cut = HALO * members
+    at = lambda r, n: slice(members * r, members * (r + n))
+    side = HALO + 4
+    loads = []
+    for step, (first, last) in enumerate(((0, 6), (8, 10), (2, 4))):
+        for low, source in ((3, first), (5, last)):
+            loads.append(
+                pltpu.make_async_copy(saved_ref.at[at(source, 2)], states[3 * step].at[at(low, 2)], in_sems.at[len(loads)])
+            )
+            loads[-1].start()
+    for n, ref, own in ((0, ks_ref, own_ks), (1, alpha_ref, own_alpha)):
+        far = slice(cut + HALO * n, cut + HALO * n + HALO)
+        ref[0:HALO] = above_ref[far]
+        ref[HALO:side] = own[0:4]
+        ref[side : side + 4] = own[rows - 4 :]
+        ref[side + 4 : 2 * side] = below_ref[far]
+    flag = slice(cut + 2 * HALO, cut + 2 * HALO + 1)
+    has_above, has_below = above_ref[flag], below_ref[flag]
+
+    def put(h, step, low, count):
+        table = low + step if low < 5 else side + low - 5 + 2 - step
+        k, g = rule(h, ks_ref, alpha_ref, table, count, members)
+        states[3 * step + 1][at(low, count)] = k
+        for j in range(count):
+            row = g[members * j : members * (j + 1)]
+            if table + j < HALO:
+                row = row * has_above
+            if table + j >= side + 4:
+                row = row * has_below
+            states[3 * step + 2][at(low + j, 1)] = row
+
+    h = [states[3 * step] for step in range(MODEL_STEPS)]
+    h[0][at(0, HALO)] = above_ref[0:cut]
+    h[0][at(7, HALO)] = below_ref[0:cut]
+    put(h[0][at(0, HALO)], 0, 0, HALO)
+    put(h[0][at(7, HALO)], 0, 7, HALO)
+    for step in range(MODEL_STEPS):
+        for n, low in enumerate((3, 5)):
+            loads[2 * step + n].wait()
+            put(h[step][at(low, 2)], step, low, 2)
+    copies = []
+    for step in range(MODEL_STEPS):
+        for low in (1, 6):
+            new = moved(*states[3 * step : 3 * step + 3], low, HALO, members, inner)
+            if step < MODEL_STEPS - 1:
+                to = 0 if low == 1 else 7
+                h[step + 1][at(to, HALO)] = new
+                put(new, step + 1, to, HALO)
+                continue
+            row = 0 if low == 1 else rows - HALO
+            h[0][at(low, HALO)] = new
+            for j in range(HALO):
+                copies.append(pltpu.make_async_copy(h[0].at[at(low + j, 1)], out_ref.at[row + j], sems.at[len(copies)]))
+                copies[-1].start()
+    for copy in copies:
+        copy.wait()
 
 
 def forecast(heads, soil_index, ks_table, alpha_table):
     members, rows, columns = heads.shape
-    halo = MODEL_STEPS
     count = lax.axis_size("dev")
-    me = lax.axis_index("dev")
-    by_row = jnp.transpose(heads, (1, 0, 2))
-    soil = soil_index.astype(jnp.float32)
-
-    def edge(lo, hi):
-        return jnp.concatenate([by_row[lo:hi].reshape(halo * members, columns), soil[lo:hi]], axis=0)
-
-    above = lax.ppermute(edge(rows - halo, rows), "dev", [(i, i + 1) for i in range(count - 1)])
-    below = lax.ppermute(edge(0, halo), "dev", [(i + 1, i) for i in range(count - 1)])
-
-    def part(block):
-        cut = halo * members
-        return block[:cut].reshape(halo, members, columns), block[cut:]
-
-    above_heads, above_soil = part(above)
-    below_heads, below_soil = part(below)
-    h = jnp.concatenate([above_heads, by_row, below_heads], axis=0)
-    kinds = jnp.concatenate([above_soil, soil, below_soil], axis=0).astype(jnp.int32)
-    ks, alpha = soil_values(kinds, ks_table, alpha_table)
-    row = jnp.arange(rows + 2 * halo)
-    inside = ((row >= halo) | (me > 0)) & ((row < rows + halo) | (me < count - 1))
-    inside = inside.astype(jnp.float32)[:, None]
-    ks = (ks * inside)[:, None, :]
-    alpha = alpha[:, None, :]
-    inside = inside[:, :, None]
-    for _ in range(MODEL_STEPS):
-        factor = jnp.exp(alpha * jnp.minimum(h, 0.0))
-        k = ks * factor
-        capacity = 0.1 + 0.4 * alpha * factor
-        flux = 0.5 * (k[1:] + k[:-1]) * (h[1:] - h[:-1])
-        mid, k_mid = h[1:-1], k[1:-1]
-        vertical = 0.5 * (k_mid[..., 1:] + k_mid[..., :-1]) * (mid[..., 1:] - mid[..., :-1] - gravity_head)
-        border = jnp.zeros_like(mid[..., :1])
-        inflow = (
-            flux[1:]
-            - flux[:-1]
-            + jnp.concatenate([vertical, border], -1)
-            - jnp.concatenate([border, vertical], -1)
-        )
-        h = (mid + step_duration * inflow / capacity[1:-1]) * inside[1:-1]
-        ks, alpha, inside = ks[1:-1], alpha[1:-1], inside[1:-1]
-    return h
+    scalars = pl.BlockSpec(memory_space=pltpu.SMEM)
+    anywhere = pl.BlockSpec(memory_space=pl.ANY)
+    whole = pl.BlockSpec(memory_space=pltpu.VMEM)
+    table_spec = pl.BlockSpec((rows, columns), lambda i: (0, 0))
+    edge_rows = HALO * members + 8
+    edge = jax.ShapeDtypeStruct((edge_rows, columns), jnp.float32)
+    table_shape = jax.ShapeDtypeStruct((rows, columns), jnp.float32)
+    edge_spec = pl.BlockSpec((edge_rows, columns), lambda i: (0, 0))
+    limit = lambda mib: pltpu.CompilerParams(vmem_limit_bytes=mib * 2**20)
+    first = pl.BlockSpec((members, 8, columns), lambda i: (0, 0, 0))
+    last = pl.BlockSpec((members, 8, columns), lambda i: (0, rows // 8 - 1, 0))
+    top, bottom, ks, alpha = pl.pallas_call(
+        edges_kernel,
+        grid=(1,),
+        out_shape=(edge, edge, table_shape, table_shape),
+        in_specs=[scalars, scalars, first, last, table_spec],
+        out_specs=(edge_spec, edge_spec, table_spec, table_spec),
+        compiler_params=limit(60),
+        name="edges",
+    )(ks_table, alpha_table, heads, heads, soil_index)
+    above = lax.ppermute(bottom, "dev", [(i, i + 1) for i in range(count - 1)])
+    below = lax.ppermute(top, "dev", [(i + 1, i) for i in range(count - 1)])
+    state = lambda r: pltpu.VMEM((r * members, columns), jnp.float32)
+    by_row = jax.ShapeDtypeStruct((rows, members, columns), jnp.float32)
+    inside, saved = pl.pallas_call(
+        interior_kernel,
+        grid=(1,),
+        out_shape=(by_row, jax.ShapeDtypeStruct((12 * members, columns), jnp.float32)),
+        in_specs=[anywhere, table_spec, table_spec],
+        out_specs=(anywhere, anywhere),
+        scratch_shapes=[pltpu.VMEM((members, rows, columns), jnp.float32)]
+        + [state(rows)] * 6
+        + [pltpu.SemaphoreType.DMA((rows,)), pltpu.SemaphoreType.DMA((rows // 8,)), pltpu.SemaphoreType.DMA((4,))],
+        compiler_params=limit(60),
+        cost_estimate=pl.CostEstimate(flops=60_000_000, bytes_accessed=5_000_000, transcendentals=4_000_000),
+        name="interior",
+    )(heads, ks, alpha)
+    return pl.pallas_call(
+        edge_kernel,
+        out_shape=by_row,
+        in_specs=[whole, whole, anywhere, whole, whole, anywhere],
+        out_specs=anywhere,
+        scratch_shapes=[state(10)] * (3 * MODEL_STEPS)
+        + [pltpu.VMEM((2 * (HALO + 4), columns), jnp.float32)] * 2
+        + [pltpu.SemaphoreType.DMA((2 * HALO,))] * 2,
+        input_output_aliases={5: 0},
+        compiler_params=limit(EDGE_MIB),
+        name="edge",
+    )(above, below, saved, ks, alpha, inside)
+
+
+def along_z(k):
+    groups, count = lax.axis_size("group"), lax.axis_size("dev")
+    top = count // 2
+    pairs = []
+    for g in range(groups):
+        for d in range(count):
+            z = (2 * (d // top) + g % 2 + k) % 4
+            pairs.append((g * count + d, (g // 2 * 2 + z % 2) * count + z // 2 * top + d % top))
+    return pairs
 
 
 def total_over_devices(x):
@@ -84,13 +263,14 @@
     x = mine + lax.ppermute(jnp.where(core == 0, high, low), "dev", other)
 
     def turned(size, base, k, n):
+        if base == 0:
+            return along_z(k)
         return [(i, i + (((i // base + k) % size) - (i // base) % size) * base) for i in range(n)]
 
     for axis, n, base, size in (
         ("dev", count, 2, 4),
         ("group", groups, 2, groups // 2),
-        ("dev", count, 8, count // 8),
-        ("group", groups, 1, 2),
+        (AXES, groups * count, 0, 4),
     ):
         arrived = [lax.ppermute(x, axis, turned(size, base, k, n)) for k in range(1, size)]
         for a in arrived:
@@ -113,18 +293,19 @@
 NN, NT, TN = ((1,), (0,)), ((1,), (1,)), ((0,), (0,))
 
 
-def gram_kernel(mask_ref, heads_ref, op_ref, values_ref, spread_ref, packed_ref, joint_ref):
-    sources, share, members, columns = heads_ref.shape
+def gram_kernel(mask_ref, op_ref, values_ref, heads_ref, spread_ref, packed_ref, joint_ref):
+    sources, share, members, columns = spread_ref.shape
     total = sources * members
     lane = lax.broadcasted_iota(jnp.int32, (OBS, 256), 1)
     for r in range(share):
-        acc = heads_ref[0, r]
+        whole = [heads_ref[s, r] for s in range(sources)]
+        acc = whole[0]
         for s in range(1, sources):
-            acc = acc + heads_ref[s, r]
+            acc = acc + whole[s]
         mean = jnp.sum(acc, axis=0, keepdims=True) / total
         parts = []
         for s in range(sources):
-            part = heads_ref[s, r] - mean
+            part = whole[s] - mean
             spread_ref[s, r] = part
             parts.append(part)
         parts.append(jnp.broadcast_to(mean, (8, columns)))
@@ -167,12 +348,12 @@
             jax.ShapeDtypeStruct(heads.shape, jnp.float32),
             jax.ShapeDtypeStruct((208, 128), jnp.float32),
         ),
-        in_specs=[pl.BlockSpec(memory_space=pltpu.SMEM), anywhere, anywhere, anywhere],
+        in_specs=[pl.BlockSpec(memory_space=pltpu.SMEM), anywhere, anywhere] + [anywhere],
         out_specs=(anywhere, anywhere),
         scratch_shapes=[pltpu.VMEM((share * BLOCKS * OBS, 256), jnp.float32)],
         compiler_params=pltpu.CompilerParams(vmem_limit_bytes=40 * 2**20),
         name="gram",
-    )(mask, heads, op, values)
+    )(mask, op, values, heads)
 
 
 def newton_kernel(packed_ref, out_ref, gram_ref):
@@ -246,10 +427,10 @@
 
 
 def body(member_pressure_heads, soil_index, ks_table, alpha_table, obs_op, obs_mask, obs_values):
-    predicted = forecast(member_pressure_heads, soil_index, ks_table, alpha_table)
-    rows, members, columns = predicted.shape
+    members, rows, columns = member_pressure_heads.shape
     groups = lax.axis_size("group")
     share = rows // groups
+    predicted = forecast(member_pressure_heads, soil_index, ks_table, alpha_table)
     heads = lax.all_to_all(predicted.reshape(groups, share, members, columns), "group", 0, 0, tiled=True)
     op = obs_op.reshape(share * BLOCKS, OBS, 128)
     values = obs_values.reshape(share * BLOCKS, OBS).T

time: 149 us -> 140 us (0.940)
  other arithmetic: 17.8 us -> 0.1 us
  Pallas kernels: 10.3 us -> 27.3 us
  starting transfers between devices: 29.3 us -> 25.1 us
  local copies, waits for them, and re-layouts: 7.02 us -> 3.01 us
  waiting for transfers between devices: 48.6 us -> 50.5 us
    pallas_call x0 -> x3, Pallas kernels: none -> 17 us  [the longest x1 10.2 us: forecast(): pl.pallas_call(interior_kernel, grid=(1,), out_shape=(by_row, jax.ShapeDt...]
    mul x13 -> x0, other arithmetic: 15.9 us -> none  [the longest x3 6.76 us: forecast(): k = ks * factor]
    ppermute x8 -> x9, starting transfers between devices: 18.7 us -> 15 us  [total_over_devices(): lax.ppermute(x, axis, turned(size, base, k, n))]
    ppermute x2, waiting for transfers between devices: 3.52 us -> 0.01 us  [the longest x1 0.01 us: forecast(): below = lax.ppermute(top, 'dev', [(i + 1, i) for i in range(count - 1)])]
    ppermute x8 -> x9, waiting for transfers between devices: 10.3 us -> 13.5 us  [total_over_devices(): lax.ppermute(x, axis, turned(size, base, k, n))]
    mul x1 -> x0, local copies, waits for them, and re-layouts: 2.77 us -> none  [forecast(): h = (mid + step_duration * inflow / capacity[1:-1]) * inside[1:-1]]
    all_to_all x1, waiting for transfers between devices: 32.6 us -> 34.9 us  [body(): lax.all_to_all(predicted.reshape(groups, share, members, columns), 'group...]
    slice x16 -> x0, local copies, waits for them, and re-layouts: 1.78 us -> none  [the longest x3 1.46 us: edge(): by_row[lo:hi].reshape(halo * members, columns)]
  transfers between devices with their start and end apart: 13 -> 14, of which waited for: 11 -> 12; matrix products, arithmetic and copies ran while one was open for 0% -> 0% of each run, Pallas kernels for 0% -> 7%
where the time goes in v2:
time: 140 us; the launch traced here: 139 us
  waiting for transfers between devices  50.5 us (36%)
  blocking collectives  33.2 us (24%)
  Pallas kernels  27.3 us (20%)
  starting transfers between devices  25.1 us (18%)
  local copies, waits for them, and re-layouts  3.01 us (2%)
    all_to_all x1, waiting for transfers between devices, body(): lax.all_to_all(predicted.reshape(groups, share, members, columns), 'group...  34.9 us
    all_to_all x1, blocking collectives, body(): back = lax.all_to_all(mixed, 'group', 0, 0, tiled=True)  33.2 us
    ppermute x9, starting transfers between devices, total_over_devices(): lax.ppermute(x, axis, turned(size, base, k, n))  15 us
    ppermute x9, waiting for transfers between devices, total_over_devices(): lax.ppermute(x, axis, turned(size, base, k, n))  13.5 us
    pallas_call x1, Pallas kernels, forecast(): pl.pallas_call(interior_kernel, grid=(1,), out_shape=(by_row, jax.ShapeDt...  10.2 us
    pallas_call x1, Pallas kernels, newton_weights(): pl.pallas_call(newton_kernel, out_shape=jax.ShapeDtypeStruct((MEMBERS, ME...  7.03 us
    all_to_all x1, starting transfers between devices, body(): lax.all_to_all(predicted.reshape(groups, share, members, columns), 'group...  6.5 us
    pallas_call x1, Pallas kernels, forecast(): pl.pallas_call(edge_kernel, out_shape=by_row, in_specs=[whole, whole, any...  4.57 us
  transfers between devices with their start and end apart: 14, of which 12 were waited for; matrix products, arithmetic and copies ran while one was open for 0% of the time, Pallas kernels for 7%

profile of v2, /device:TPU:0, one launch (start us, length us, event | category | flops | bytes accessed | tf_op | source)
XLA Modules:
  0.0 139.3 jit_solution(11788247497244231147)
XLA Ops:
  0.0 2.2 %edges.1 = (f32[80,768]{1,0:T(8,128)}, f32[80,768]{1,0:T(8,128)}, f32[32,768]{1,0:T(8,128)}, f32[32,768]{1,0:T(8,128)}) custom-call(f32[8]{0:T(128)} %ks_table.1, f32[8]{0:T(128)} %alpha_table.1, f32[24,32,768]{2,1,0:T(8,128)} %heads_ref.1, f32[24,32,768]{2,1,0:T(8,128)} %heads_ref.1, s32[32,768]{1,0:T(8,128)} %soil_ref.1), custom_call_target="tpu_custom_call" | custom-call | tf_op jit(solution)/shard_map/edges/pallas_call | solution.py:204
  2.2 1.3 collective-permute-start
  3.5 1.3 collective-permute-start.1
  4.8 10.2 %interior.1 = (f32[32,24,768]{2,1,0:T(8,128)}, f32[288,768]{1,0:T(8,128)}) custom-call(f32[24,32,768]{2,1,0:T(8,128)} %heads_ref.1, f32[32,768]{1,0:T(8,128)} %get-tuple-element.15.ks_ref.own_ks, f32[32,768]{1,0:T(8,128)} %get-tuple-element.16.alpha_ref.own_alpha), custom_call_target="tpu_custom_call" | custom-call | flops 60000000 | bytes 5000000 | tf_op jit(solution)/shard_map/interior/pallas_call | solution.py:217
  15.8 4.6 %edge.1 = f32[32,24,768]{2,1,0:T(8,128)} custom-call(f32[80,768]{1,0:T(8,128)} %copy-done.2, f32[80,768]{1,0:T(8,128)} %copy-done.3, f32[288,768]{1,0:T(8,128)} %get-tuple-element.17.saved_ref, f32[32,768]{1,0:T(8,128)} %get-tuple-element.15.ks_ref.own_ks, f32[32,768]{1,0:T(8,128)} %get-tuple-element.16.alpha_ref.own_alpha, ...), custom_call_target="tpu_custom_call", output_to_operand_aliasing={{}: (5, {})} | custom-call | tf_op jit(solution)/shard_map/edge/pallas_call | solution.py:230
  20.4 6.5 %all-to-all-start = ((f32[8,4,24,768]{3,2,1,0:T(8,128)}), f32[8,4,24,768]{3,2,1,0:T(8,128)S(1)}, u32[]{:S(2)}, u32[]{:S(2)}) async-start(f32[8,4,24,768]{3,2,1,0:T(8,128)} %bitcast.9), calls=%async_computation | async-start | bytes 4718592 | tf_op jit(solution)/shard_map/all_to_all | solution.py:434
  27.0 34.9 %all-to-all-done.heads_ref = f32[8,4,24,768]{3,2,1,0:T(8,128)S(1)} async-done(((f32[8,4,24,768]{3,2,1,0:T(8,128)}), f32[8,4,24,768]{3,2,1,0:T(8,128)S(1)}, u32[]{:S(2)}, u32[]{:S(2)}) %all-to-all-start) | async-done | bytes 2359328 | tf_op jit(solution)/shard_map/all_to_all | solution.py:434
  61.9 2.2 %gram.1 = (f32[8,4,24,768]{3,2,1,0:T(8,128)S(1)}, f32[208,128]{1,0:T(8,128)S(1)}) custom-call(s32[4,6]{1,0:T(4,128)S(1)} %copy-done.1, f32[24,32,128]{2,1,0:T(8,128)S(1)} %bitcast.7, f32[32,24]{1,0:T(8,128)S(1)} %bitcast.8, f32[8,4,24,768]{3,2,1,0:T(8,128)S(1)} %all-to-all-done.heads_ref), custom_call_target="tpu_custom_call" | custom-call | tf_op jit(solution)/shard_map/gram/pallas_call | solution.py:345
  64.1 1.0 collective-permute-start.2
  66.0 3.7 %collective-permute-start.3 = (f32[104,128]{1,0:T(8,128)S(1)}, f32[104,128]{1,0:T(8,128)S(1)}, u32[]{:S(2)}, u32[]{:S(2)}) collective-permute-start(f32[104,128]{1,0:T(8,128)S(1)} %select_add_fusion), channel_id=1, source_target_pairs={{0,2},{1,3},{2,4},{3,5},{4,6},{5,7},{6,0},{7,1},{8,10},{9,11},{10,... | collective-permute-start | bytes 159752 | tf_op jit(solution)/shard_map/ppermute | solution.py:275
  69.7 3.8 %collective-permute-start.4 = (f32[104,128]{1,0:T(8,128)S(1)}, f32[104,128]{1,0:T(8,128)S(1)}, u32[]{:S(2)}, u32[]{:S(2)}) collective-permute-start(f32[104,128]{1,0:T(8,128)S(1)} %select_add_fusion), channel_id=1, source_target_pairs={{0,4},{1,5},{2,6},{3,7},{4,0},{5,1},{6,2},{7,3},{8,12},{9,13},{10,... | collective-permute-start | bytes 159752 | tf_op jit(solution)/shard_map/ppermute | solution.py:275
  74.2 2.3 %collective-permute-done.4 = f32[104,128]{1,0:T(8,128)S(1)} collective-permute-done((f32[104,128]{1,0:T(8,128)S(1)}, f32[104,128]{1,0:T(8,128)S(1)}, u32[]{:S(2)}, u32[]{:S(2)}) %collective-permute-start.4) | collective-permute-done | bytes 53280 | tf_op jit(solution)/shard_map/ppermute | solution.py:275
  76.5 1.1 collective-permute-done.5
  78.2 2.7 %collective-permute-start.7 = (f32[104,128]{1,0:T(8,128)S(1)}, f32[104,128]{1,0:T(8,128)S(1)}, u32[]{:S(2)}, u32[]{:S(2)}) collective-permute-start(f32[104,128]{1,0:T(8,128)S(1)} %add_add_fusion.2), channel_id=1, source_target_pairs={{0,64},{16,80},{32,96},{48,112},{64,0},{80,16},{96,32},{112,48},{1... | collective-permute-start | bytes 159752 | tf_op jit(solution)/shard_map/ppermute | solution.py:275
  81.0 2.1 %collective-permute-done.6 = f32[104,128]{1,0:T(8,128)S(1)} collective-permute-done((f32[104,128]{1,0:T(8,128)S(1)}, f32[104,128]{1,0:T(8,128)S(1)}, u32[]{:S(2)}, u32[]{:S(2)}) %collective-permute-start.6) | collective-permute-done | bytes 53280 | tf_op jit(solution)/shard_map/ppermute | solution.py:275
  83.8 1.2 collective-permute-done.8
  85.9 3.3 %collective-permute-start.11 = (f32[104,128]{1,0:T(8,128)S(1)}, f32[104,128]{1,0:T(8,128)S(1)}, u32[]{:S(2)}, u32[]{:S(2)}) collective-permute-start(f32[104,128]{1,0:T(8,128)S(1)} %add_add_fusion.1), channel_id=1, source_target_pairs={{0,24},{1,25},{2,26},{3,27},{4,28},{5,29},{6,30},{7,31},{8,16},{9,... | collective-permute-start | bytes 159752 | tf_op jit(solution)/shard_map/ppermute | solution.py:275
  89.2 1.7 %collective-permute-done.10 = f32[104,128]{1,0:T(8,128)S(1)} collective-permute-done((f32[104,128]{1,0:T(8,128)S(1)}, f32[104,128]{1,0:T(8,128)S(1)}, u32[]{:S(2)}, u32[]{:S(2)}) %collective-permute-start.10) | collective-permute-done | bytes 53280 | tf_op jit(solution)/shard_map/ppermute | solution.py:275
  91.0 3.6 %collective-permute-done.9 = f32[104,128]{1,0:T(8,128)S(1)} collective-permute-done((f32[104,128]{1,0:T(8,128)S(1)}, f32[104,128]{1,0:T(8,128)S(1)}, u32[]{:S(2)}, u32[]{:S(2)}) %collective-permute-start.9) | collective-permute-done | bytes 53280 | tf_op jit(solution)/shard_map/ppermute | solution.py:275
  94.6 1.2 collective-permute-done.12
  95.9 7.0 %newton.1.weights_ref = f32[192,192]{1,0:T(8,128)S(1)} custom-call(f32[208,128]{1,0:T(8,128)S(1)} %pad_maximum_fusion.packed_ref), custom_call_target="tpu_custom_call" | custom-call | tf_op jit(solution)/shard_map/newton/pallas_call | solution.py:395
  102.9 1.1 mix.1
  104.0 33.2 %all_to_all.10 = f32[8,4,24,768]{3,2,1,0:T(8,128)S(1)} all-to-all(f32[8,4,24,768]{3,2,1,0:T(8,128)S(1)} %mix.1), channel_id=1, replica_groups=mesh['group'=8,'dev'=16] {'group'}, dimensions={0} | all-to-all | bytes 4718592 | tf_op jit(solution)/shard_map/all_to_all | solution.py:439
  137.2 2.1 %copy.15 = f32[32,24,768]{2,0,1:T(8,128)} copy(f32[32,24,768]{2,1,0:T(8,128)S(1)} %bitcast.10) | data formatting | bytes 4718592 | tf_op jit(solution)/shard_map/reshape | solution.py:440
  (32 shorter events, 4.9 us)
Async XLA Ops:
  2.2 12.8 %collective-permute-start = (f32[80,768]{1,0:T(8,128)}, f32[80,768]{1,0:T(8,128)S(1)}, u32[]{:S(2)}, u32[]{:S(2)}) collective-permute-start(f32[80,768]{1,0:T(8,128)} %get-tuple-element.13), channel_id=1, source_target_pairs={{0,1},{1,2},{2,3},{3,4},{4,5},{5,6},{6,7},{7,8},{8,9},{9,10},{10,1... | collective-permute-start | bytes 737288 | tf_op jit(solution)/shard_map/ppermute | solution.py:213
  3.5 11.5 %collective-permute-start.1 = (f32[80,768]{1,0:T(8,128)}, f32[80,768]{1,0:T(8,128)S(1)}, u32[]{:S(2)}, u32[]{:S(2)}) collective-permute-start(f32[80,768]{1,0:T(8,128)} %get-tuple-element.14), channel_id=1, source_target_pairs={{1,0},{2,1},{3,2},{4,3},{5,4},{6,5},{7,6},{8,7},{9,8},{10,9},{11,1... | collective-permute-start | bytes 737288 | tf_op jit(solution)/shard_map/ppermute | solution.py:214
  15.0 0.7 copy-start.2
  15.0 0.8 copy-start.3
  20.4 6.5 %copy-start.4 = (f32[4,6,32]{2,0,1:T(4,128)S(1)}, f32[4,6,32]{2,0,1:T(4,128)}, u32[]{:S(2)}) copy-start(f32[4,6,32]{2,0,1:T(4,128)} %param.13) | copy-start | bytes 9220
  20.4 41.5 %copy-start = (f32[4,6,32,128]{3,2,1,0:T(8,128)S(1)}, f32[4,6,32,128]{3,2,1,0:T(8,128)}, u32[]{:S(2)}) copy-start(f32[4,6,32,128]{3,2,1,0:T(8,128)} %param.11) | copy-start | bytes 1179652
  20.4 41.5 %copy-start.1 = (s32[4,6]{1,0:T(4,128)S(1)}, s32[4,6]{1,0:T(4,128)}, u32[]{:S(2)}) copy-start(s32[4,6]{1,0:T(4,128)} %mask_ref.1) | copy-start | bytes 292
  20.4 41.5 %all-to-all-start = ((f32[8,4,24,768]{3,2,1,0:T(8,128)}), f32[8,4,24,768]{3,2,1,0:T(8,128)S(1)}, u32[]{:S(2)}, u32[]{:S(2)}) async-start(f32[8,4,24,768]{3,2,1,0:T(8,128)} %bitcast.9), calls=%async_computation | async-start | bytes 4718592 | tf_op jit(solution)/shard_map/all_to_all | solution.py:434
  64.1 1.9 %collective-permute-start.2 = (f32[104,128]{1,0:T(8,128)S(1)}, f32[104,128]{1,0:T(8,128)S(1)}, u32[]{:S(2)}, u32[]{:S(2)}) collective-permute-start(f32[104,128]{1,0:T(8,128)S(1)} %slice_select_fusion), channel_id=1, source_target_pairs={{0,1},{1,0},{2,3},{3,2},{4,5},{5,4},{6,7},{7,6},{8,9},{9,8},{10,11... | collective-permute-start | bytes 159752 | tf_op jit(solution)/shard_map/ppermute | solution.py:263
  66.0 8.2 %collective-permute-start.3 = (f32[104,128]{1,0:T(8,128)S(1)}, f32[104,128]{1,0:T(8,128)S(1)}, u32[]{:S(2)}, u32[]{:S(2)}) collective-permute-start(f32[104,128]{1,0:T(8,128)S(1)} %select_add_fusion), channel_id=1, source_target_pairs={{0,2},{1,3},{2,4},{3,5},{4,6},{5,7},{6,0},{7,1},{8,10},{9,11},{10,... | collective-permute-start | bytes 159752 | tf_op jit(solution)/shard_map/ppermute | solution.py:275
  69.7 6.8 %collective-permute-start.4 = (f32[104,128]{1,0:T(8,128)S(1)}, f32[104,128]{1,0:T(8,128)S(1)}, u32[]{:S(2)}, u32[]{:S(2)}) collective-permute-start(f32[104,128]{1,0:T(8,128)S(1)} %select_add_fusion), channel_id=1, source_target_pairs={{0,4},{1,5},{2,6},{3,7},{4,0},{5,1},{6,2},{7,3},{8,12},{9,13},{10,... | collective-permute-start | bytes 159752 | tf_op jit(solution)/shard_map/ppermute | solution.py:275
  73.5 4.1 %collective-permute-start.5 = (f32[104,128]{1,0:T(8,128)S(1)}, f32[104,128]{1,0:T(8,128)S(1)}, u32[]{:S(2)}, u32[]{:S(2)}) collective-permute-start(f32[104,128]{1,0:T(8,128)S(1)} %select_add_fusion), channel_id=1, source_target_pairs={{0,6},{1,7},{2,0},{3,1},{4,2},{5,3},{6,4},{7,5},{8,14},{9,15},{10,... | collective-permute-start | bytes 159752 | tf_op jit(solution)/shard_map/ppermute | solution.py:275
  77.6 5.4 %collective-permute-start.6 = (f32[104,128]{1,0:T(8,128)S(1)}, f32[104,128]{1,0:T(8,128)S(1)}, u32[]{:S(2)}, u32[]{:S(2)}) collective-permute-start(f32[104,128]{1,0:T(8,128)S(1)} %add_add_fusion.2), channel_id=1, source_target_pairs={{0,32},{16,48},{32,64},{48,80},{64,96},{80,112},{96,0},{112,16},{1... | collective-permute-start | bytes 159752 | tf_op jit(solution)/shard_map/ppermute | solution.py:275
  78.2 5.6 %collective-permute-start.7 = (f32[104,128]{1,0:T(8,128)S(1)}, f32[104,128]{1,0:T(8,128)S(1)}, u32[]{:S(2)}, u32[]{:S(2)}) collective-permute-start(f32[104,128]{1,0:T(8,128)S(1)} %add_add_fusion.2), channel_id=1, source_target_pairs={{0,64},{16,80},{32,96},{48,112},{64,0},{80,16},{96,32},{112,48},{1... | collective-permute-start | bytes 159752 | tf_op jit(solution)/shard_map/ppermute | solution.py:275
  80.9 4.1 %collective-permute-start.8 = (f32[104,128]{1,0:T(8,128)S(1)}, f32[104,128]{1,0:T(8,128)S(1)}, u32[]{:S(2)}, u32[]{:S(2)}) collective-permute-start(f32[104,128]{1,0:T(8,128)S(1)} %add_add_fusion.2), channel_id=1, source_target_pairs={{0,96},{16,112},{32,0},{48,16},{64,32},{80,48},{96,64},{112,80},{1... | collective-permute-start | bytes 159752 | tf_op jit(solution)/shard_map/ppermute | solution.py:275
  85.0 5.8 %collective-permute-start.10 = (f32[104,128]{1,0:T(8,128)S(1)}, f32[104,128]{1,0:T(8,128)S(1)}, u32[]{:S(2)}, u32[]{:S(2)}) collective-permute-start(f32[104,128]{1,0:T(8,128)S(1)} %add_add_fusion.1), channel_id=1, source_target_pairs={{0,8},{1,9},{2,10},{3,11},{4,12},{5,13},{6,14},{7,15},{8,0},{9,1},... | collective-permute-start | bytes 159752 | tf_op jit(solution)/shard_map/ppermute | solution.py:275
  85.9 5.1 %collective-permute-start.11 = (f32[104,128]{1,0:T(8,128)S(1)}, f32[104,128]{1,0:T(8,128)S(1)}, u32[]{:S(2)}, u32[]{:S(2)}) collective-permute-start(f32[104,128]{1,0:T(8,128)S(1)} %add_add_fusion.1), channel_id=1, source_target_pairs={{0,24},{1,25},{2,26},{3,27},{4,28},{5,29},{6,30},{7,31},{8,16},{9,... | collective-permute-start | bytes 159752 | tf_op jit(solution)/shard_map/ppermute | solution.py:275
  89.2 5.3 %collective-permute-start.9 = (f32[104,128]{1,0:T(8,128)S(1)}, f32[104,128]{1,0:T(8,128)S(1)}, u32[]{:S(2)}, u32[]{:S(2)}) collective-permute-start(f32[104,128]{1,0:T(8,128)S(1)} %add_add_fusion.1), channel_id=1, source_target_pairs={{0,16},{1,17},{2,18},{3,19},{4,20},{5,21},{6,22},{7,23},{8,24},{9,... | collective-permute-start | bytes 159752 | tf_op jit(solution)/shard_map/ppermute | solution.py:275
  94.5 1.3 collective-permute-start.12

commit v3 on v2

--- a/solution.py
+++ b/solution.py
@@ -15,23 +15,41 @@
 HALO = MODEL_STEPS
 LN2 = 0.6931471805599453
 UNROLL = 4
-EDGE_MIB = 60
+FORECAST_MIB = 32
 gravity_head = 1.0
 AXES = ("group", "dev")
 
 
-def edges_kernel(ks_table, alpha_table, first_ref, last_ref, soil_ref, top_ref, bottom_ref, ks_ref, alpha_ref):
-    members, span, columns = first_ref.shape
+def edges_kernel(ks_far, alpha_far, heads_ref, soil_far, top_ref, bottom_ref, tables_ref, ks_table, alpha_table, soil_ref, first, last, sems):
+    members, span, columns = first.shape
     rows = soil_ref.shape[0]
+    loads = [
+        pltpu.make_async_copy(source, ref, sems.at[n])
+        for n, (source, ref) in enumerate(
+            (
+                (ks_far, ks_table),
+                (alpha_far, alpha_table),
+                (soil_far, soil_ref),
+                (heads_ref.at[:, 0:span], first),
+                (heads_ref.at[:, rows - span : rows], last),
+            )
+        )
+    ]
+    for load in loads:
+        load.start()
+    for load in loads[:3]:
+        load.wait()
     ks, alpha = soil_tables(soil_ref[...], ks_table, alpha_table)
-    ks_ref[...] = ks
-    alpha_ref[...] = alpha
+    tables_ref[0:rows] = ks
+    tables_ref[rows:] = alpha
     flag = jnp.ones((8 - 2 * HALO, columns), jnp.float32)
-    for j in range(HALO):
-        top_ref[members * j : members * j + members] = first_ref[:, j, :]
-        bottom_ref[members * j : members * j + members] = last_ref[:, span - HALO + j, :]
     top_ref[HALO * members :] = jnp.concatenate([ks[:HALO], alpha[:HALO], flag], 0)
     bottom_ref[HALO * members :] = jnp.concatenate([ks[rows - HALO :], alpha[rows - HALO :], flag], 0)
+    for load in loads[3:]:
+        load.wait()
+    for j in range(HALO):
+        top_ref[members * j : members * j + members] = first[:, j, :]
+        bottom_ref[members * j : members * j + members] = last[:, span - HALO + j, :]
 
 
 def law(h, ks, alpha, slope):
@@ -78,8 +96,9 @@
     return (lax.broadcasted_iota(jnp.int32, (1, 128), 1) < 127).astype(jnp.float32)
 
 
-def interior_kernel(heads_ref, ks_ref, alpha_ref, out_ref, saved_ref, given, h0, h1, k0, k1, g0, g1, sems, in_sems, save_sems):
+def interior_kernel(heads_ref, tables_ref, out_ref, saved_ref, given, h0, h1, k0, k1, g0, g1, sems, in_sems, save_sems):
     members, rows, columns = given.shape
+    ks_ref, alpha_ref = tables_ref.at[0:rows], tables_ref.at[rows:]
     tile = 8
     loads = [
         pltpu.make_async_copy(heads_ref.at[:, t : t + tile], given.at[:, t : t + tile], in_sems.at[t // tile])
@@ -123,27 +142,20 @@
         copy.wait()
 
 
-def edge_kernel(above_ref, below_ref, saved_ref, own_ks, own_alpha, given_ref, out_ref, *scratch):
+def edge_kernel(above_ref, below_ref, saved_ref, tables_ref, given_ref, out_ref, *scratch):
     del given_ref
-    *states, ks_ref, alpha_ref, sems, in_sems = scratch
-    rows, columns = own_ks.shape
+    *states, ks_ref, alpha_ref, sems = scratch
+    rows = tables_ref.shape[0] // 2
     members = saved_ref.shape[0] // 12
     inner = inner_mask()
     cut = HALO * members
     at = lambda r, n: slice(members * r, members * (r + n))
     side = HALO + 4
-    loads = []
-    for step, (first, last) in enumerate(((0, 6), (8, 10), (2, 4))):
-        for low, source in ((3, first), (5, last)):
-            loads.append(
-                pltpu.make_async_copy(saved_ref.at[at(source, 2)], states[3 * step].at[at(low, 2)], in_sems.at[len(loads)])
-            )
-            loads[-1].start()
-    for n, ref, own in ((0, ks_ref, own_ks), (1, alpha_ref, own_alpha)):
+    for n, ref in ((0, ks_ref), (1, alpha_ref)):
         far = slice(cut + HALO * n, cut + HALO * n + HALO)
         ref[0:HALO] = above_ref[far]
-        ref[HALO:side] = own[0:4]
-        ref[side : side + 4] = own[rows - 4 :]
+        ref[HALO:side] = tables_ref[rows * n : rows * n + 4]
+        ref[side : side + 4] = tables_ref[rows * n + rows - 4 : rows * n + rows]
         ref[side + 4 : 2 * side] = below_ref[far]
     flag = slice(cut + 2 * HALO, cut + 2 * HALO + 1)
     has_above, has_below = above_ref[flag], below_ref[flag]
@@ -166,9 +178,10 @@
     put(h[0][at(0, HALO)], 0, 0, HALO)
     put(h[0][at(7, HALO)], 0, 7, HALO)
     for step in range(MODEL_STEPS):
-        for n, low in enumerate((3, 5)):
-            loads[2 * step + n].wait()
-            put(h[step][at(low, 2)], step, low, 2)
+        for low, source in zip((3, 5), ((0, 6), (8, 10), (2, 4))[step]):
+            kept = saved_ref[at(source, 2)]
+            h[step][at(low, 2)] = kept
+            put(kept, step, low, 2)
     copies = []
     for step in range(MODEL_STEPS):
         for low in (1, 6):
@@ -190,55 +203,50 @@
 def forecast(heads, soil_index, ks_table, alpha_table):
     members, rows, columns = heads.shape
     count = lax.axis_size("dev")
-    scalars = pl.BlockSpec(memory_space=pltpu.SMEM)
-    anywhere = pl.BlockSpec(memory_space=pl.ANY)
-    whole = pl.BlockSpec(memory_space=pltpu.VMEM)
-    table_spec = pl.BlockSpec((rows, columns), lambda i: (0, 0))
-    edge_rows = HALO * members + 8
-    edge = jax.ShapeDtypeStruct((edge_rows, columns), jnp.float32)
-    table_shape = jax.ShapeDtypeStruct((rows, columns), jnp.float32)
-    edge_spec = pl.BlockSpec((edge_rows, columns), lambda i: (0, 0))
+    far = pl.BlockSpec(memory_space=pltpu.HBM)
+    near = pl.BlockSpec(memory_space=pltpu.VMEM)
+    edge = jax.ShapeDtypeStruct((HALO * members + 8, columns), jnp.float32)
+    table = jax.ShapeDtypeStruct((2 * rows, columns), jnp.float32)
+    block = pltpu.VMEM((members, 8, columns), jnp.float32)
     limit = lambda mib: pltpu.CompilerParams(vmem_limit_bytes=mib * 2**20)
-    first = pl.BlockSpec((members, 8, columns), lambda i: (0, 0, 0))
-    last = pl.BlockSpec((members, 8, columns), lambda i: (0, rows // 8 - 1, 0))
-    top, bottom, ks, alpha = pl.pallas_call(
+    top, bottom, tables = pl.pallas_call(
         edges_kernel,
-        grid=(1,),
-        out_shape=(edge, edge, table_shape, table_shape),
-        in_specs=[scalars, scalars, first, last, table_spec],
-        out_specs=(edge_spec, edge_spec, table_spec, table_spec),
+        out_shape=(edge, edge, table),
+        in_specs=[far] * 4,
+        out_specs=(near, near, near),
+        scratch_shapes=[pltpu.SMEM((SOIL_TYPES,), jnp.float32)] * 2
+        + [pltpu.VMEM((rows, columns), jnp.int32), block, block, pltpu.SemaphoreType.DMA((5,))],
         compiler_params=limit(60),
         name="edges",
-    )(ks_table, alpha_table, heads, heads, soil_index)
+    )(ks_table, alpha_table, heads, soil_index)
     above = lax.ppermute(bottom, "dev", [(i, i + 1) for i in range(count - 1)])
     below = lax.ppermute(top, "dev", [(i + 1, i) for i in range(count - 1)])
     state = lambda r: pltpu.VMEM((r * members, columns), jnp.float32)
     by_row = jax.ShapeDtypeStruct((rows, members, columns), jnp.float32)
     inside, saved = pl.pallas_call(
         interior_kernel,
-        grid=(1,),
         out_shape=(by_row, jax.ShapeDtypeStruct((12 * members, columns), jnp.float32)),
-        in_specs=[anywhere, table_spec, table_spec],
-        out_specs=(anywhere, anywhere),
+        in_specs=[far, near],
+        out_specs=(far, near),
         scratch_shapes=[pltpu.VMEM((members, rows, columns), jnp.float32)]
         + [state(rows)] * 6
         + [pltpu.SemaphoreType.DMA((rows,)), pltpu.SemaphoreType.DMA((rows // 8,)), pltpu.SemaphoreType.DMA((4,))],
-        compiler_params=limit(60),
+        compiler_params=limit(FORECAST_MIB),
         cost_estimate=pl.CostEstimate(flops=60_000_000, bytes_accessed=5_000_000, transcendentals=4_000_000),
         name="interior",
-    )(heads, ks, alpha)
+    )(heads, tables)
     return pl.pallas_call(
         edge_kernel,
         out_shape=by_row,
-        in_specs=[whole, whole, anywhere, whole, whole, anywhere],
-        out_specs=anywhere,
+        in_specs=[near] * 4 + [far],
+        out_specs=far,
         scratch_shapes=[state(10)] * (3 * MODEL_STEPS)
         + [pltpu.VMEM((2 * (HALO + 4), columns), jnp.float32)] * 2
-        + [pltpu.SemaphoreType.DMA((2 * HALO,))] * 2,
-        input_output_aliases={5: 0},
-        compiler_params=limit(EDGE_MIB),
+        + [pltpu.SemaphoreType.DMA((2 * HALO,))],
+        input_output_aliases={4: 0},
+        compiler_params=limit(FORECAST_MIB),
         name="edge",
-    )(above, below, saved, ks, alpha, inside)
+    )(above, below, saved, tables, inside)
 
 
 def along_z(k):

time: 140 us -> 137 us (0.979)
  Pallas kernels: 27.3 us -> 24.2 us
    pallas_call x3, Pallas kernels: 17 us -> 14 us  [the longest x1 9.37 us: forecast(): pl.pallas_call(interior_kernel, out_shape=(by_row, jax.ShapeDtypeStruct((...]
where the time goes in v3:
time: 137 us; the launch traced here: 136 us
  waiting for transfers between devices  50.5 us (37%)
  blocking collectives  33.2 us (24%)
  starting transfers between devices  25.1 us (18%)
  Pallas kernels  24.2 us (18%)
  local copies, waits for them, and re-layouts  3.15 us (2%)
    all_to_all x1, waiting for transfers between devices, body(): lax.all_to_all(predicted.reshape(groups, share, members, columns), 'group...  34.9 us
    all_to_all x1, blocking collectives, body(): back = lax.all_to_all(mixed, 'group', 0, 0, tiled=True)  33.2 us
    ppermute x9, starting transfers between devices, total_over_devices(): lax.ppermute(x, axis, turned(size, base, k, n))  14.8 us
    ppermute x9, waiting for transfers between devices, total_over_devices(): lax.ppermute(x, axis, turned(size, base, k, n))  13.5 us
    pallas_call x1, Pallas kernels, forecast(): pl.pallas_call(interior_kernel, out_shape=(by_row, jax.ShapeDtypeStruct((...  9.37 us
    pallas_call x1, Pallas kernels, newton_weights(): pl.pallas_call(newton_kernel, out_shape=jax.ShapeDtypeStruct((MEMBERS, ME...  7.03 us
    all_to_all x1, starting transfers between devices, body(): lax.all_to_all(predicted.reshape(groups, share, members, columns), 'group...  6.5 us
  transfers between devices with their start and end apart: 14, of which 12 were waited for; matrix products, arithmetic and copies ran while one was open for 0% of the time, Pallas kernels for 7%

profile of v3, /device:TPU:0, one launch (start us, length us, event | category | flops | bytes accessed | tf_op | source)
XLA Modules:
  0.0 136.5 jit_solution(13452375217965119040)
XLA Ops:
  0.0 2.4 %edges.1 = (f32[80,768]{1,0:T(8,128)}, f32[80,768]{1,0:T(8,128)}, f32[64,768]{1,0:T(8,128)}) custom-call(f32[8]{0:T(128)} %ks_far.1, f32[8]{0:T(128)} %alpha_far.1, f32[24,32,768]{2,1,0:T(8,128)} %heads_ref.3, s32[32,768]{1,0:T(8,128)} %soil_far.1), custom_call_target="tpu_custom_call" | custom-call | tf_op jit(solution)/shard_map/edges/pallas_call | solution.py:212
  2.4 1.3 collective-permute-start
  3.7 1.3 collective-permute-start.1
  6.0 9.4 %interior.1 = (f32[32,24,768]{2,1,0:T(8,128)}, f32[288,768]{1,0:T(8,128)S(1)}) custom-call(f32[24,32,768]{2,1,0:T(8,128)S(1)} %copy-done, f32[64,768]{1,0:T(8,128)S(1)} %copy-done.2), custom_call_target="tpu_custom_call" | custom-call | flops 60000000 | bytes 5000000 | tf_op jit(solution)/shard_map/interior/pallas_call | solution.py:226
  15.4 2.2 %edge.1 = f32[32,24,768]{2,1,0:T(8,128)} custom-call(f32[80,768]{1,0:T(8,128)S(1)} %collective-permute-done.above_ref, f32[80,768]{1,0:T(8,128)S(1)} %collective-permute-done.1.below_ref, f32[288,768]{1,0:T(8,128)S(1)} %get-tuple-element.15.saved_ref, f32[64,768]{1,0:T(8,128)S(1)} %copy-done.2, ...), custom_call_target="tpu_custom_call", output_to_operand_aliasing={{}: (4, {})} | custom-call | tf_op jit(solution)/shard_map/edge/pallas_call | solution.py:238
  17.6 6.5 %all-to-all-start = ((f32[8,4,24,768]{3,2,1,0:T(8,128)}), f32[8,4,24,768]{3,2,1,0:T(8,128)S(1)}, u32[]{:S(2)}, u32[]{:S(2)}) async-start(f32[8,4,24,768]{3,2,1,0:T(8,128)} %bitcast.2), calls=%async_computation | async-start | bytes 4718592 | tf_op jit(solution)/shard_map/all_to_all | solution.py:442
  24.2 34.9 %all-to-all-done.heads_ref = f32[8,4,24,768]{3,2,1,0:T(8,128)S(1)} async-done(((f32[8,4,24,768]{3,2,1,0:T(8,128)}), f32[8,4,24,768]{3,2,1,0:T(8,128)S(1)}, u32[]{:S(2)}, u32[]{:S(2)}) %all-to-all-start) | async-done | bytes 2359328 | tf_op jit(solution)/shard_map/all_to_all | solution.py:442
  59.1 2.1 %gram.1 = (f32[8,4,24,768]{3,2,1,0:T(8,128)S(1)}, f32[208,128]{1,0:T(8,128)S(1)}) custom-call(s32[4,6]{1,0:T(4,128)S(1)} %copy-done.3, f32[24,32,128]{2,1,0:T(8,128)S(1)} %bitcast.7, f32[32,24]{1,0:T(8,128)S(1)} %bitcast.8, f32[8,4,24,768]{3,2,1,0:T(8,128)S(1)} %all-to-all-done.heads_ref), custom_call_target="tpu_custom_call" | custom-call | tf_op jit(solution)/shard_map/gram/pallas_call | solution.py:353
  61.3 1.1 collective-permute-start.2
  63.3 3.5 %collective-permute-start.3 = (f32[104,128]{1,0:T(8,128)S(1)}, f32[104,128]{1,0:T(8,128)S(1)}, u32[]{:S(2)}, u32[]{:S(2)}) collective-permute-start(f32[104,128]{1,0:T(8,128)S(1)} %select_add_fusion), channel_id=1, source_target_pairs={{0,2},{1,3},{2,4},{3,5},{4,6},{5,7},{6,0},{7,1},{8,10},{9,11},{10,... | collective-permute-start | bytes 159752 | tf_op jit(solution)/shard_map/ppermute | solution.py:283
  66.8 3.8 %collective-permute-start.4 = (f32[104,128]{1,0:T(8,128)S(1)}, f32[104,128]{1,0:T(8,128)S(1)}, u32[]{:S(2)}, u32[]{:S(2)}) collective-permute-start(f32[104,128]{1,0:T(8,128)S(1)} %select_add_fusion), channel_id=1, source_target_pairs={{0,4},{1,5},{2,6},{3,7},{4,0},{5,1},{6,2},{7,3},{8,12},{9,13},{10,... | collective-permute-start | bytes 159752 | tf_op jit(solution)/shard_map/ppermute | solution.py:283
  71.3 2.3 %collective-permute-done.4 = f32[104,128]{1,0:T(8,128)S(1)} collective-permute-done((f32[104,128]{1,0:T(8,128)S(1)}, f32[104,128]{1,0:T(8,128)S(1)}, u32[]{:S(2)}, u32[]{:S(2)}) %collective-permute-start.4) | collective-permute-done | bytes 53280 | tf_op jit(solution)/shard_map/ppermute | solution.py:283
  73.6 1.1 collective-permute-done.5
  75.3 2.7 %collective-permute-start.7 = (f32[104,128]{1,0:T(8,128)S(1)}, f32[104,128]{1,0:T(8,128)S(1)}, u32[]{:S(2)}, u32[]{:S(2)}) collective-permute-start(f32[104,128]{1,0:T(8,128)S(1)} %add_add_fusion.2), channel_id=1, source_target_pairs={{0,64},{16,80},{32,96},{48,112},{64,0},{80,16},{96,32},{112,48},{1... | collective-permute-start | bytes 159752 | tf_op jit(solution)/shard_map/ppermute | solution.py:283
  78.1 2.1 %collective-permute-done.6 = f32[104,128]{1,0:T(8,128)S(1)} collective-permute-done((f32[104,128]{1,0:T(8,128)S(1)}, f32[104,128]{1,0:T(8,128)S(1)}, u32[]{:S(2)}, u32[]{:S(2)}) %collective-permute-start.6) | collective-permute-done | bytes 53280 | tf_op jit(solution)/shard_map/ppermute | solution.py:283
  80.9 1.2 collective-permute-done.8
  83.0 3.3 %collective-permute-start.11 = (f32[104,128]{1,0:T(8,128)S(1)}, f32[104,128]{1,0:T(8,128)S(1)}, u32[]{:S(2)}, u32[]{:S(2)}) collective-permute-start(f32[104,128]{1,0:T(8,128)S(1)} %add_add_fusion.1), channel_id=1, source_target_pairs={{0,24},{1,25},{2,26},{3,27},{4,28},{5,29},{6,30},{7,31},{8,16},{9,... | collective-permute-start | bytes 159752 | tf_op jit(solution)/shard_map/ppermute | solution.py:283
  86.3 1.7 %collective-permute-done.10 = f32[104,128]{1,0:T(8,128)S(1)} collective-permute-done((f32[104,128]{1,0:T(8,128)S(1)}, f32[104,128]{1,0:T(8,128)S(1)}, u32[]{:S(2)}, u32[]{:S(2)}) %collective-permute-start.10) | collective-permute-done | bytes 53280 | tf_op jit(solution)/shard_map/ppermute | solution.py:283
  88.1 3.6 %collective-permute-done.9 = f32[104,128]{1,0:T(8,128)S(1)} collective-permute-done((f32[104,128]{1,0:T(8,128)S(1)}, f32[104,128]{1,0:T(8,128)S(1)}, u32[]{:S(2)}, u32[]{:S(2)}) %collective-permute-start.9) | collective-permute-done | bytes 53280 | tf_op jit(solution)/shard_map/ppermute | solution.py:283
  91.8 1.2 collective-permute-done.12
  93.0 7.0 %newton.1.weights_ref = f32[192,192]{1,0:T(8,128)S(1)} custom-call(f32[208,128]{1,0:T(8,128)S(1)} %pad_maximum_fusion.packed_ref), custom_call_target="tpu_custom_call" | custom-call | tf_op jit(solution)/shard_map/newton/pallas_call | solution.py:403
  100.1 1.1 mix.1
  101.2 33.2 %all_to_all.10 = f32[8,4,24,768]{3,2,1,0:T(8,128)S(1)} all-to-all(f32[8,4,24,768]{3,2,1,0:T(8,128)S(1)} %mix.1), channel_id=1, replica_groups=mesh['group'=8,'dev'=16] {'group'}, dimensions={0} | all-to-all | bytes 4718592 | tf_op jit(solution)/shard_map/all_to_all | solution.py:447
  134.3 2.1 %copy.15 = f32[32,24,768]{2,0,1:T(8,128)} copy(f32[32,24,768]{2,1,0:T(8,128)S(1)} %bitcast.9) | data formatting | bytes 4718592 | tf_op jit(solution)/shard_map/reshape | solution.py:448
  (32 shorter events, 5.1 us)
Async XLA Ops:
  0.0 5.0 %copy-start = (f32[24,32,768]{2,1,0:T(8,128)S(1)}, f32[24,32,768]{2,1,0:T(8,128)}, u32[]{:S(2)}) copy-start(f32[24,32,768]{2,1,0:T(8,128)} %heads_ref.3) | copy-start | bytes 7077892
  2.4 12.9 %collective-permute-start = (f32[80,768]{1,0:T(8,128)}, f32[80,768]{1,0:T(8,128)S(1)}, u32[]{:S(2)}, u32[]{:S(2)}) collective-permute-start(f32[80,768]{1,0:T(8,128)} %get-tuple-element.12), channel_id=1, source_target_pairs={{0,1},{1,2},{2,3},{3,4},{4,5},{5,6},{6,7},{7,8},{8,9},{9,10},{10,1... | collective-permute-start | bytes 737288 | tf_op jit(solution)/shard_map/ppermute | solution.py:222
  3.7 11.6 %collective-permute-start.1 = (f32[80,768]{1,0:T(8,128)}, f32[80,768]{1,0:T(8,128)S(1)}, u32[]{:S(2)}, u32[]{:S(2)}) collective-permute-start(f32[80,768]{1,0:T(8,128)} %get-tuple-element.13), channel_id=1, source_target_pairs={{1,0},{2,1},{3,2},{4,3},{5,4},{6,5},{7,6},{8,7},{9,8},{10,9},{11,1... | collective-permute-start | bytes 737288 | tf_op jit(solution)/shard_map/ppermute | solution.py:223
  5.0 0.9 copy-start.2
  17.6 6.5 %copy-start.4 = (f32[4,6,32]{2,0,1:T(4,128)S(1)}, f32[4,6,32]{2,0,1:T(4,128)}, u32[]{:S(2)}) copy-start(f32[4,6,32]{2,0,1:T(4,128)} %param.13) | copy-start | bytes 9220
  17.6 41.5 %copy-start.1 = (f32[4,6,32,128]{3,2,1,0:T(8,128)S(1)}, f32[4,6,32,128]{3,2,1,0:T(8,128)}, u32[]{:S(2)}) copy-start(f32[4,6,32,128]{3,2,1,0:T(8,128)} %param.11) | copy-start | bytes 1179652
  17.6 41.5 %copy-start.3 = (s32[4,6]{1,0:T(4,128)S(1)}, s32[4,6]{1,0:T(4,128)}, u32[]{:S(2)}) copy-start(s32[4,6]{1,0:T(4,128)} %mask_ref.1) | copy-start | bytes 292
  17.6 41.5 %all-to-all-start = ((f32[8,4,24,768]{3,2,1,0:T(8,128)}), f32[8,4,24,768]{3,2,1,0:T(8,128)S(1)}, u32[]{:S(2)}, u32[]{:S(2)}) async-start(f32[8,4,24,768]{3,2,1,0:T(8,128)} %bitcast.2), calls=%async_computation | async-start | bytes 4718592 | tf_op jit(solution)/shard_map/all_to_all | solution.py:442
  61.3 2.0 %collective-permute-start.2 = (f32[104,128]{1,0:T(8,128)S(1)}, f32[104,128]{1,0:T(8,128)S(1)}, u32[]{:S(2)}, u32[]{:S(2)}) collective-permute-start(f32[104,128]{1,0:T(8,128)S(1)} %slice_select_fusion), channel_id=1, source_target_pairs={{0,1},{1,0},{2,3},{3,2},{4,5},{5,4},{6,7},{7,6},{8,9},{9,8},{10,11... | collective-permute-start | bytes 159752 | tf_op jit(solution)/shard_map/ppermute | solution.py:271
  63.3 8.0 %collective-permute-start.3 = (f32[104,128]{1,0:T(8,128)S(1)}, f32[104,128]{1,0:T(8,128)S(1)}, u32[]{:S(2)}, u32[]{:S(2)}) collective-permute-start(f32[104,128]{1,0:T(8,128)S(1)} %select_add_fusion), channel_id=1, source_target_pairs={{0,2},{1,3},{2,4},{3,5},{4,6},{5,7},{6,0},{7,1},{8,10},{9,11},{10,... | collective-permute-start | bytes 159752 | tf_op jit(solution)/shard_map/ppermute | solution.py:283
  66.8 6.8 %collective-permute-start.4 = (f32[104,128]{1,0:T(8,128)S(1)}, f32[104,128]{1,0:T(8,128)S(1)}, u32[]{:S(2)}, u32[]{:S(2)}) collective-permute-start(f32[104,128]{1,0:T(8,128)S(1)} %select_add_fusion), channel_id=1, source_target_pairs={{0,4},{1,5},{2,6},{3,7},{4,0},{5,1},{6,2},{7,3},{8,12},{9,13},{10,... | collective-permute-start | bytes 159752 | tf_op jit(solution)/shard_map/ppermute | solution.py:283
  70.6 4.1 %collective-permute-start.5 = (f32[104,128]{1,0:T(8,128)S(1)}, f32[104,128]{1,0:T(8,128)S(1)}, u32[]{:S(2)}, u32[]{:S(2)}) collective-permute-start(f32[104,128]{1,0:T(8,128)S(1)} %select_add_fusion), channel_id=1, source_target_pairs={{0,6},{1,7},{2,0},{3,1},{4,2},{5,3},{6,4},{7,5},{8,14},{9,15},{10,... | collective-permute-start | bytes 159752 | tf_op jit(solution)/shard_map/ppermute | solution.py:283
  74.8 5.4 %collective-permute-start.6 = (f32[104,128]{1,0:T(8,128)S(1)}, f32[104,128]{1,0:T(8,128)S(1)}, u32[]{:S(2)}, u32[]{:S(2)}) collective-permute-start(f32[104,128]{1,0:T(8,128)S(1)} %add_add_fusion.2), channel_id=1, source_target_pairs={{0,32},{16,48},{32,64},{48,80},{64,96},{80,112},{96,0},{112,16},{1... | collective-permute-start | bytes 159752 | tf_op jit(solution)/shard_map/ppermute | solution.py:283
  75.3 5.6 %collective-permute-start.7 = (f32[104,128]{1,0:T(8,128)S(1)}, f32[104,128]{1,0:T(8,128)S(1)}, u32[]{:S(2)}, u32[]{:S(2)}) collective-permute-start(f32[104,128]{1,0:T(8,128)S(1)} %add_add_fusion.2), channel_id=1, source_target_pairs={{0,64},{16,80},{32,96},{48,112},{64,0},{80,16},{96,32},{112,48},{1... | collective-permute-start | bytes 159752 | tf_op jit(solution)/shard_map/ppermute | solution.py:283
  78.0 4.1 %collective-permute-start.8 = (f32[104,128]{1,0:T(8,128)S(1)}, f32[104,128]{1,0:T(8,128)S(1)}, u32[]{:S(2)}, u32[]{:S(2)}) collective-permute-start(f32[104,128]{1,0:T(8,128)S(1)} %add_add_fusion.2), channel_id=1, source_target_pairs={{0,96},{16,112},{32,0},{48,16},{64,32},{80,48},{96,64},{112,80},{1... | collective-permute-start | bytes 159752 | tf_op jit(solution)/shard_map/ppermute | solution.py:283
  82.1 5.8 %collective-permute-start.10 = (f32[104,128]{1,0:T(8,128)S(1)}, f32[104,128]{1,0:T(8,128)S(1)}, u32[]{:S(2)}, u32[]{:S(2)}) collective-permute-start(f32[104,128]{1,0:T(8,128)S(1)} %add_add_fusion.1), channel_id=1, source_target_pairs={{0,8},{1,9},{2,10},{3,11},{4,12},{5,13},{6,14},{7,15},{8,0},{9,1},... | collective-permute-start | bytes 159752 | tf_op jit(solution)/shard_map/ppermute | solution.py:283
  83.0 5.1 %collective-permute-start.11 = (f32[104,128]{1,0:T(8,128)S(1)}, f32[104,128]{1,0:T(8,128)S(1)}, u32[]{:S(2)}, u32[]{:S(2)}) collective-permute-start(f32[104,128]{1,0:T(8,128)S(1)} %add_add_fusion.1), channel_id=1, source_target_pairs={{0,24},{1,25},{2,26},{3,27},{4,28},{5,29},{6,30},{7,31},{8,16},{9,... | collective-permute-start | bytes 159752 | tf_op jit(solution)/shard_map/ppermute | solution.py:283
  86.3 5.3 %collective-permute-start.9 = (f32[104,128]{1,0:T(8,128)S(1)}, f32[104,128]{1,0:T(8,128)S(1)}, u32[]{:S(2)}, u32[]{:S(2)}) collective-permute-start(f32[104,128]{1,0:T(8,128)S(1)} %add_add_fusion.1), channel_id=1, source_target_pairs={{0,16},{1,17},{2,18},{3,19},{4,20},{5,21},{6,22},{7,23},{8,24},{9,... | collective-permute-start | bytes 159752 | tf_op jit(solution)/shard_map/ppermute | solution.py:283
  91.7 1.3 collective-permute-start.12

commit v4 on v3

--- a/solution.py
+++ b/solution.py
@@ -340,11 +340,15 @@
     both = halves(joint_ref[...])
     gram = product(both, both, TN)
     side = lax.broadcasted_iota(jnp.int32, (64, 128), 1)
-    packed_ref[0:64] = jnp.where(side < 64, gram[0:64, :128], gram[64:128, :128])
-    packed_ref[64:128] = jnp.where(side < 64, gram[64:128, :128], pltpu.roll(gram[128:192, 128:], 64, 1))
-    packed_ref[128:192] = gram[128:192, :128]
-    packed_ref[192:200] = gram[192:200, :128]
-    packed_ref[200:208] = gram[192:200, 128:]
+    down = lax.broadcasted_iota(jnp.int32, (64, 128), 0)
+    turned = pltpu.roll(gram[64:128, :128], 64, 1)
+    corner = pltpu.roll(gram[128:192, 128:], 64, 1)
+    packed_ref[0:64] = jnp.where(side < 64, jnp.where(down >= side, gram[0:64, :128], turned), corner)
+    packed_ref[64:128] = gram[128:192, :128]
+    packed_ref[128:160] = jnp.where(side[:32] < 64, gram[64:96, :128], turned[32:])
+    packed_ref[160:168] = gram[192:200, :128]
+    diagonal = jnp.sum(jnp.where(down + 64 == side, gram[64:128, :128], 0.0), axis=0, keepdims=True)
+    packed_ref[168:176] = jnp.where(side[:8] < 64, gram[192:200, 128:], jnp.broadcast_to(diagonal, (8, 128)))
 
 
 def mean_and_gram(heads, op, mask, values):
@@ -354,7 +358,7 @@
         gram_kernel,
         out_shape=(
             jax.ShapeDtypeStruct(heads.shape, jnp.float32),
-            jax.ShapeDtypeStruct((208, 128), jnp.float32),
+            jax.ShapeDtypeStruct((176, 128), jnp.float32),
         ),
         in_specs=[pl.BlockSpec(memory_space=pltpu.SMEM), anywhere, anywhere] + [anywhere],
         out_specs=(anywhere, anywhere),
@@ -367,20 +371,23 @@
 def newton_kernel(packed_ref, out_ref, gram_ref):
     order = MEMBERS
     side = lax.broadcasted_iota(jnp.int32, (64, 128), 1)
-    p0, p1, p2 = packed_ref[0:64], packed_ref[64:128], packed_ref[128:192]
-    below = jnp.where(side < 64, p1, p0)
-    turned = jnp.concatenate([p0, below], 0).T
-    gram_ref[0:64, 0:128] = jnp.where(side < 64, p0, turned[0:64])
-    gram_ref[64:128, 0:128] = below
-    gram_ref[128:192, 0:128] = p2
-    gram_ref[0:128, 128:192] = p2.T
-    gram_ref[128:192, 128:192] = pltpu.roll(p1, 64, 1)[:, :64]
+    down = lax.broadcasted_iota(jnp.int32, (64, 128), 0)
+    p0, p1, p2 = packed_ref[0:64], packed_ref[64:128], packed_ref[128:160]
+    lower = jnp.concatenate([p2, pltpu.roll(p2, 64, 1)], 0)
+    turned = jnp.concatenate([p0, lower], 0).T[0:64]
+    diagonal = jnp.broadcast_to(pltpu.roll(packed_ref[168:176], 64, 1)[0:1], (64, 128))
+    second = jnp.where(down < side, p0, jnp.where(down == side, diagonal, turned))
+    gram_ref[0:64, 0:128] = jnp.where((side < 64) & (down >= side), p0, turned)
+    gram_ref[64:128, 0:128] = jnp.where(side < 64, lower, pltpu.roll(second, 64, 1))
+    gram_ref[128:192, 0:128] = p1
+    gram_ref[0:128, 128:192] = p1.T
+    gram_ref[128:192, 128:192] = pltpu.roll(p0, 64, 1)[:, :64]
     eye = (
         lax.broadcasted_iota(jnp.int32, (order, order), 0)
         == lax.broadcasted_iota(jnp.int32, (order, order), 1)
     ).astype(jnp.float32)
     gram = gram_ref[...] + (MEMBERS - 1.0) * eye
-    rhs = jnp.concatenate([packed_ref[192:200], packed_ref[200:208, :64]], 1)
+    rhs = jnp.concatenate([packed_ref[160:168], packed_ref[168:176, :64]], 1)
     norm = jnp.sum(jnp.abs(gram), keepdims=True)
     inverse_norm = 1.0 / norm
     iterate = gram * inverse_norm

time: 137 us -> 136 us (level)
  no operation moved by 1% of the time
where the time goes in v4:
time: 136 us
  waiting for transfers between devices  50.2 us (37%)
  blocking collectives  33.1 us (24%)
  starting transfers between devices  25.1 us (18%)
  Pallas kernels  24.3 us (18%)
  local copies, waits for them, and re-layouts  3.15 us (2%)
    all_to_all x1, waiting for transfers between devices, body(): lax.all_to_all(predicted.reshape(groups, share, members, columns), 'group...  34.9 us
    all_to_all x1, blocking collectives, body(): back = lax.all_to_all(mixed, 'group', 0, 0, tiled=True)  33.1 us
    ppermute x9, starting transfers between devices, total_over_devices(): lax.ppermute(x, axis, turned(size, base, k, n))  14.7 us
    ppermute x9, waiting for transfers between devices, total_over_devices(): lax.ppermute(x, axis, turned(size, base, k, n))  13.3 us
    pallas_call x1, Pallas kernels, forecast(): pl.pallas_call(interior_kernel, out_shape=(by_row, jax.ShapeDtypeStruct((...  9.37 us
    pallas_call x1, Pallas kernels, newton_weights(): pl.pallas_call(newton_kernel, out_shape=jax.ShapeDtypeStruct((MEMBERS, ME...  7.1 us
    all_to_all x1, starting transfers between devices, body(): lax.all_to_all(predicted.reshape(groups, share, members, columns), 'group...  6.5 us
  transfers between devices with their start and end apart: 14, of which 12 were waited for; matrix products, arithmetic and copies ran while one was open for 0% of the time, Pallas kernels for 7%

profile of v4, /device:TPU:0, one launch (start us, length us, event | category | flops | bytes accessed | tf_op | source)
XLA Modules:
  0.0 136.1 jit_solution(13945129294823970246)
XLA Ops:
  0.0 2.4 %edges.1 = (f32[80,768]{1,0:T(8,128)}, f32[80,768]{1,0:T(8,128)}, f32[64,768]{1,0:T(8,128)}) custom-call(f32[8]{0:T(128)} %ks_far.1, f32[8]{0:T(128)} %alpha_far.1, f32[24,32,768]{2,1,0:T(8,128)} %heads_ref.3, s32[32,768]{1,0:T(8,128)} %soil_far.1), custom_call_target="tpu_custom_call" | custom-call | tf_op jit(solution)/shard_map/edges/pallas_call | solution.py:212
  2.4 1.3 collective-permute-start
  3.7 1.3 collective-permute-start.1
  6.0 9.4 %interior.1 = (f32[32,24,768]{2,1,0:T(8,128)}, f32[288,768]{1,0:T(8,128)S(1)}) custom-call(f32[24,32,768]{2,1,0:T(8,128)S(1)} %copy-done, f32[64,768]{1,0:T(8,128)S(1)} %copy-done.2), custom_call_target="tpu_custom_call" | custom-call | flops 60000000 | bytes 5000000 | tf_op jit(solution)/shard_map/interior/pallas_call | solution.py:226
  15.4 2.2 %edge.1 = f32[32,24,768]{2,1,0:T(8,128)} custom-call(f32[80,768]{1,0:T(8,128)S(1)} %collective-permute-done.above_ref, f32[80,768]{1,0:T(8,128)S(1)} %collective-permute-done.1.below_ref, f32[288,768]{1,0:T(8,128)S(1)} %get-tuple-element.15.saved_ref, f32[64,768]{1,0:T(8,128)S(1)} %copy-done.2, ...), custom_call_target="tpu_custom_call", output_to_operand_aliasing={{}: (4, {})} | custom-call | tf_op jit(solution)/shard_map/edge/pallas_call | solution.py:238
  17.6 6.5 %all-to-all-start = ((f32[8,4,24,768]{3,2,1,0:T(8,128)}), f32[8,4,24,768]{3,2,1,0:T(8,128)S(1)}, u32[]{:S(2)}, u32[]{:S(2)}) async-start(f32[8,4,24,768]{3,2,1,0:T(8,128)} %bitcast.2), calls=%async_computation | async-start | bytes 4718592 | tf_op jit(solution)/shard_map/all_to_all | solution.py:449
  24.2 34.9 %all-to-all-done.heads_ref = f32[8,4,24,768]{3,2,1,0:T(8,128)S(1)} async-done(((f32[8,4,24,768]{3,2,1,0:T(8,128)}), f32[8,4,24,768]{3,2,1,0:T(8,128)S(1)}, u32[]{:S(2)}, u32[]{:S(2)}) %all-to-all-start) | async-done | bytes 2359328 | tf_op jit(solution)/shard_map/all_to_all | solution.py:449
  59.1 2.1 %gram.1 = (f32[8,4,24,768]{3,2,1,0:T(8,128)S(1)}, f32[176,128]{1,0:T(8,128)S(1)}) custom-call(s32[4,6]{1,0:T(4,128)S(1)} %copy-done.3, f32[24,32,128]{2,1,0:T(8,128)S(1)} %bitcast.7, f32[32,24]{1,0:T(8,128)S(1)} %bitcast.8, f32[8,4,24,768]{3,2,1,0:T(8,128)S(1)} %all-to-all-done.heads_ref), custom_call_target="tpu_custom_call" | custom-call | tf_op jit(solution)/shard_map/gram/pallas_call | solution.py:357
  61.3 1.1 collective-permute-start.2
  63.3 3.5 %collective-permute-start.3 = (f32[88,128]{1,0:T(8,128)S(1)}, f32[88,128]{1,0:T(8,128)S(1)}, u32[]{:S(2)}, u32[]{:S(2)}) collective-permute-start(f32[88,128]{1,0:T(8,128)S(1)} %select_add_fusion), channel_id=1, source_target_pairs={{0,2},{1,3},{2,4},{3,5},{4,6},{5,7},{6,0},{7,1},{8,10},{9,11},{10,... | collective-permute-start | bytes 135176 | tf_op jit(solution)/shard_map/ppermute | solution.py:283
  66.8 3.8 %collective-permute-start.4 = (f32[88,128]{1,0:T(8,128)S(1)}, f32[88,128]{1,0:T(8,128)S(1)}, u32[]{:S(2)}, u32[]{:S(2)}) collective-permute-start(f32[88,128]{1,0:T(8,128)S(1)} %select_add_fusion), channel_id=1, source_target_pairs={{0,4},{1,5},{2,6},{3,7},{4,0},{5,1},{6,2},{7,3},{8,12},{9,13},{10,... | collective-permute-start | bytes 135176 | tf_op jit(solution)/shard_map/ppermute | solution.py:283
  71.2 2.1 %collective-permute-done.4 = f32[88,128]{1,0:T(8,128)S(1)} collective-permute-done((f32[88,128]{1,0:T(8,128)S(1)}, f32[88,128]{1,0:T(8,128)S(1)}, u32[]{:S(2)}, u32[]{:S(2)}) %collective-permute-start.4) | collective-permute-done | bytes 45088 | tf_op jit(solution)/shard_map/ppermute | solution.py:283
  73.3 1.4 %collective-permute-done.5 = f32[88,128]{1,0:T(8,128)S(1)} collective-permute-done((f32[88,128]{1,0:T(8,128)S(1)}, f32[88,128]{1,0:T(8,128)S(1)}, u32[]{:S(2)}, u32[]{:S(2)}) %collective-permute-start.5) | collective-permute-done | bytes 45088 | tf_op jit(solution)/shard_map/ppermute | solution.py:283
  75.2 2.7 %collective-permute-start.7 = (f32[88,128]{1,0:T(8,128)S(1)}, f32[88,128]{1,0:T(8,128)S(1)}, u32[]{:S(2)}, u32[]{:S(2)}) collective-permute-start(f32[88,128]{1,0:T(8,128)S(1)} %add_add_fusion.2), channel_id=1, source_target_pairs={{0,64},{16,80},{32,96},{48,112},{64,0},{80,16},{96,32},{112,48},{1... | collective-permute-start | bytes 135176 | tf_op jit(solution)/shard_map/ppermute | solution.py:283
  78.0 2.0 %collective-permute-done.6 = f32[88,128]{1,0:T(8,128)S(1)} collective-permute-done((f32[88,128]{1,0:T(8,128)S(1)}, f32[88,128]{1,0:T(8,128)S(1)}, u32[]{:S(2)}, u32[]{:S(2)}) %collective-permute-start.6) | collective-permute-done | bytes 45088 | tf_op jit(solution)/shard_map/ppermute | solution.py:283
  80.7 1.2 collective-permute-done.8
  82.7 3.4 %collective-permute-start.11 = (f32[88,128]{1,0:T(8,128)S(1)}, f32[88,128]{1,0:T(8,128)S(1)}, u32[]{:S(2)}, u32[]{:S(2)}) collective-permute-start(f32[88,128]{1,0:T(8,128)S(1)} %add_add_fusion.1), channel_id=1, source_target_pairs={{0,24},{1,25},{2,26},{3,27},{4,28},{5,29},{6,30},{7,31},{8,16},{9,... | collective-permute-start | bytes 135176 | tf_op jit(solution)/shard_map/ppermute | solution.py:283
  86.1 1.5 %collective-permute-done.10 = f32[88,128]{1,0:T(8,128)S(1)} collective-permute-done((f32[88,128]{1,0:T(8,128)S(1)}, f32[88,128]{1,0:T(8,128)S(1)}, u32[]{:S(2)}, u32[]{:S(2)}) %collective-permute-start.10) | collective-permute-done | bytes 45088 | tf_op jit(solution)/shard_map/ppermute | solution.py:283
  87.8 3.5 %collective-permute-done.9 = f32[88,128]{1,0:T(8,128)S(1)} collective-permute-done((f32[88,128]{1,0:T(8,128)S(1)}, f32[88,128]{1,0:T(8,128)S(1)}, u32[]{:S(2)}, u32[]{:S(2)}) %collective-permute-start.9) | collective-permute-done | bytes 45088 | tf_op jit(solution)/shard_map/ppermute | solution.py:283
  91.4 1.2 collective-permute-done.12
  92.7 7.1 %newton.1.weights_ref = f32[192,192]{1,0:T(8,128)S(1)} custom-call(f32[176,128]{1,0:T(8,128)S(1)} %pad_maximum_fusion.packed_ref), custom_call_target="tpu_custom_call" | custom-call | tf_op jit(solution)/shard_map/newton/pallas_call | solution.py:410
  99.8 1.1 mix.1
  100.9 33.1 %all_to_all.10 = f32[8,4,24,768]{3,2,1,0:T(8,128)S(1)} all-to-all(f32[8,4,24,768]{3,2,1,0:T(8,128)S(1)} %mix.1), channel_id=1, replica_groups=mesh['group'=8,'dev'=16] {'group'}, dimensions={0} | all-to-all | bytes 4718592 | tf_op jit(solution)/shard_map/all_to_all | solution.py:454
  134.0 2.1 %copy.15 = f32[32,24,768]{2,0,1:T(8,128)} copy(f32[32,24,768]{2,1,0:T(8,128)S(1)} %bitcast.9) | data formatting | bytes 4718592 | tf_op jit(solution)/shard_map/reshape | solution.py:455
  (32 shorter events, 4.9 us)
Async XLA Ops:
  0.0 5.0 %copy-start = (f32[24,32,768]{2,1,0:T(8,128)S(1)}, f32[24,32,768]{2,1,0:T(8,128)}, u32[]{:S(2)}) copy-start(f32[24,32,768]{2,1,0:T(8,128)} %heads_ref.3) | copy-start | bytes 7077892
  2.4 12.9 %collective-permute-start = (f32[80,768]{1,0:T(8,128)}, f32[80,768]{1,0:T(8,128)S(1)}, u32[]{:S(2)}, u32[]{:S(2)}) collective-permute-start(f32[80,768]{1,0:T(8,128)} %get-tuple-element.12), channel_id=1, source_target_pairs={{0,1},{1,2},{2,3},{3,4},{4,5},{5,6},{6,7},{7,8},{8,9},{9,10},{10,1... | collective-permute-start | bytes 737288 | tf_op jit(solution)/shard_map/ppermute | solution.py:222
  3.7 11.6 %collective-permute-start.1 = (f32[80,768]{1,0:T(8,128)}, f32[80,768]{1,0:T(8,128)S(1)}, u32[]{:S(2)}, u32[]{:S(2)}) collective-permute-start(f32[80,768]{1,0:T(8,128)} %get-tuple-element.13), channel_id=1, source_target_pairs={{1,0},{2,1},{3,2},{4,3},{5,4},{6,5},{7,6},{8,7},{9,8},{10,9},{11,1... | collective-permute-start | bytes 737288 | tf_op jit(solution)/shard_map/ppermute | solution.py:223
  5.0 0.9 copy-start.2
  17.6 6.5 %copy-start.4 = (f32[4,6,32]{2,0,1:T(4,128)S(1)}, f32[4,6,32]{2,0,1:T(4,128)}, u32[]{:S(2)}) copy-start(f32[4,6,32]{2,0,1:T(4,128)} %param.13) | copy-start | bytes 9220
  17.6 41.5 %copy-start.1 = (f32[4,6,32,128]{3,2,1,0:T(8,128)S(1)}, f32[4,6,32,128]{3,2,1,0:T(8,128)}, u32[]{:S(2)}) copy-start(f32[4,6,32,128]{3,2,1,0:T(8,128)} %param.11) | copy-start | bytes 1179652
  17.6 41.5 %copy-start.3 = (s32[4,6]{1,0:T(4,128)S(1)}, s32[4,6]{1,0:T(4,128)}, u32[]{:S(2)}) copy-start(s32[4,6]{1,0:T(4,128)} %mask_ref.1) | copy-start | bytes 292
  17.6 41.5 %all-to-all-start = ((f32[8,4,24,768]{3,2,1,0:T(8,128)}), f32[8,4,24,768]{3,2,1,0:T(8,128)S(1)}, u32[]{:S(2)}, u32[]{:S(2)}) async-start(f32[8,4,24,768]{3,2,1,0:T(8,128)} %bitcast.2), calls=%async_computation | async-start | bytes 4718592 | tf_op jit(solution)/shard_map/all_to_all | solution.py:449
  61.3 2.0 %collective-permute-start.2 = (f32[88,128]{1,0:T(8,128)S(1)}, f32[88,128]{1,0:T(8,128)S(1)}, u32[]{:S(2)}, u32[]{:S(2)}) collective-permute-start(f32[88,128]{1,0:T(8,128)S(1)} %slice_select_fusion), channel_id=1, source_target_pairs={{0,1},{1,0},{2,3},{3,2},{4,5},{5,4},{6,7},{7,6},{8,9},{9,8},{10,11... | collective-permute-start | bytes 135176 | tf_op jit(solution)/shard_map/ppermute | solution.py:271
  63.3 7.9 %collective-permute-start.3 = (f32[88,128]{1,0:T(8,128)S(1)}, f32[88,128]{1,0:T(8,128)S(1)}, u32[]{:S(2)}, u32[]{:S(2)}) collective-permute-start(f32[88,128]{1,0:T(8,128)S(1)} %select_add_fusion), channel_id=1, source_target_pairs={{0,2},{1,3},{2,4},{3,5},{4,6},{5,7},{6,0},{7,1},{8,10},{9,11},{10,... | collective-permute-start | bytes 135176 | tf_op jit(solution)/shard_map/ppermute | solution.py:283
  66.8 6.5 %collective-permute-start.4 = (f32[88,128]{1,0:T(8,128)S(1)}, f32[88,128]{1,0:T(8,128)S(1)}, u32[]{:S(2)}, u32[]{:S(2)}) collective-permute-start(f32[88,128]{1,0:T(8,128)S(1)} %select_add_fusion), channel_id=1, source_target_pairs={{0,4},{1,5},{2,6},{3,7},{4,0},{5,1},{6,2},{7,3},{8,12},{9,13},{10,... | collective-permute-start | bytes 135176 | tf_op jit(solution)/shard_map/ppermute | solution.py:283
  70.6 4.0 %collective-permute-start.5 = (f32[88,128]{1,0:T(8,128)S(1)}, f32[88,128]{1,0:T(8,128)S(1)}, u32[]{:S(2)}, u32[]{:S(2)}) collective-permute-start(f32[88,128]{1,0:T(8,128)S(1)} %select_add_fusion), channel_id=1, source_target_pairs={{0,6},{1,7},{2,0},{3,1},{4,2},{5,3},{6,4},{7,5},{8,14},{9,15},{10,... | collective-permute-start | bytes 135176 | tf_op jit(solution)/shard_map/ppermute | solution.py:283
  74.7 5.3 %collective-permute-start.6 = (f32[88,128]{1,0:T(8,128)S(1)}, f32[88,128]{1,0:T(8,128)S(1)}, u32[]{:S(2)}, u32[]{:S(2)}) collective-permute-start(f32[88,128]{1,0:T(8,128)S(1)} %add_add_fusion.2), channel_id=1, source_target_pairs={{0,32},{16,48},{32,64},{48,80},{64,96},{80,112},{96,0},{112,16},{1... | collective-permute-start | bytes 135176 | tf_op jit(solution)/shard_map/ppermute | solution.py:283
  75.2 5.6 %collective-permute-start.7 = (f32[88,128]{1,0:T(8,128)S(1)}, f32[88,128]{1,0:T(8,128)S(1)}, u32[]{:S(2)}, u32[]{:S(2)}) collective-permute-start(f32[88,128]{1,0:T(8,128)S(1)} %add_add_fusion.2), channel_id=1, source_target_pairs={{0,64},{16,80},{32,96},{48,112},{64,0},{80,16},{96,32},{112,48},{1... | collective-permute-start | bytes 135176 | tf_op jit(solution)/shard_map/ppermute | solution.py:283
  77.9 4.0 %collective-permute-start.8 = (f32[88,128]{1,0:T(8,128)S(1)}, f32[88,128]{1,0:T(8,128)S(1)}, u32[]{:S(2)}, u32[]{:S(2)}) collective-permute-start(f32[88,128]{1,0:T(8,128)S(1)} %add_add_fusion.2), channel_id=1, source_target_pairs={{0,96},{16,112},{32,0},{48,16},{64,32},{80,48},{96,64},{112,80},{1... | collective-permute-start | bytes 135176 | tf_op jit(solution)/shard_map/ppermute | solution.py:283
  82.0 5.6 %collective-permute-start.10 = (f32[88,128]{1,0:T(8,128)S(1)}, f32[88,128]{1,0:T(8,128)S(1)}, u32[]{:S(2)}, u32[]{:S(2)}) collective-permute-start(f32[88,128]{1,0:T(8,128)S(1)} %add_add_fusion.1), channel_id=1, source_target_pairs={{0,8},{1,9},{2,10},{3,11},{4,12},{5,13},{6,14},{7,15},{8,0},{9,1},... | collective-permute-start | bytes 135176 | tf_op jit(solution)/shard_map/ppermute | solution.py:283
  82.7 5.1 %collective-permute-start.11 = (f32[88,128]{1,0:T(8,128)S(1)}, f32[88,128]{1,0:T(8,128)S(1)}, u32[]{:S(2)}, u32[]{:S(2)}) collective-permute-start(f32[88,128]{1,0:T(8,128)S(1)} %add_add_fusion.1), channel_id=1, source_target_pairs={{0,24},{1,25},{2,26},{3,27},{4,28},{5,29},{6,30},{7,31},{8,16},{9,... | collective-permute-start | bytes 135176 | tf_op jit(solution)/shard_map/ppermute | solution.py:283
  86.1 5.3 %collective-permute-start.9 = (f32[88,128]{1,0:T(8,128)S(1)}, f32[88,128]{1,0:T(8,128)S(1)}, u32[]{:S(2)}, u32[]{:S(2)}) collective-permute-start(f32[88,128]{1,0:T(8,128)S(1)} %add_add_fusion.1), channel_id=1, source_target_pairs={{0,16},{1,17},{2,18},{3,19},{4,20},{5,21},{6,22},{7,23},{8,24},{9,... | collective-permute-start | bytes 135176 | tf_op jit(solution)/shard_map/ppermute | solution.py:283
  91.4 1.3 collective-permute-start.12

commit v5 on v4

--- a/solution.py
+++ b/solution.py
@@ -276,9 +276,9 @@
         return [(i, i + (((i // base + k) % size) - (i // base) % size) * base) for i in range(n)]
 
     for axis, n, base, size in (
+        (AXES, groups * count, 0, 4),
+        ("group", groups, 2, groups // 2),
         ("dev", count, 2, 4),
-        ("group", groups, 2, groups // 2),
-        (AXES, groups * count, 0, 4),
     ):
         arrived = [lax.ppermute(x, axis, turned(size, base, k, n)) for k in range(1, size)]
         for a in arrived:

time: 136 us -> 135 us (level)
  waiting for transfers between devices: 50.2 us -> 46.9 us
  starting transfers between devices: 25.1 us -> 26.5 us
    ppermute x9, waiting for transfers between devices: 13.3 us -> 9.89 us  [total_over_devices(): lax.ppermute(x, axis, turned(size, base, k, n))]
    ppermute x9, starting transfers between devices: 14.7 us -> 16.2 us  [total_over_devices(): lax.ppermute(x, axis, turned(size, base, k, n))]
  transfers between devices with their start and end apart: 14 -> 14, of which waited for: 12 -> 11; matrix products, arithmetic and copies ran while one was open for 0% -> 0% of each run, Pallas kernels for 7% -> 7%
where the time goes in v5:
time: 135 us
  waiting for transfers between devices  46.9 us (35%)
  blocking collectives  33.8 us (25%)
  starting transfers between devices  26.5 us (20%)
  Pallas kernels  24.3 us (18%)
  local copies, waits for them, and re-layouts  3.15 us (2%)
    all_to_all x1, waiting for transfers between devices, body(): lax.all_to_all(predicted.reshape(groups, share, members, columns), 'group...  34.9 us
    all_to_all x1, blocking collectives, body(): back = lax.all_to_all(mixed, 'group', 0, 0, tiled=True)  33.8 us
    ppermute x9, starting transfers between devices, total_over_devices(): lax.ppermute(x, axis, turned(size, base, k, n))  16.2 us
    ppermute x9, waiting for transfers between devices, total_over_devices(): lax.ppermute(x, axis, turned(size, base, k, n))  9.89 us
    pallas_call x1, Pallas kernels, forecast(): pl.pallas_call(interior_kernel, out_shape=(by_row, jax.ShapeDtypeStruct((...  9.37 us
    pallas_call x1, Pallas kernels, newton_weights(): pl.pallas_call(newton_kernel, out_shape=jax.ShapeDtypeStruct((MEMBERS, ME...  7.1 us
    all_to_all x1, starting transfers between devices, body(): lax.all_to_all(predicted.reshape(groups, share, members, columns), 'group...  6.5 us
  transfers between devices with their start and end apart: 14, of which 11 were waited for; matrix products, arithmetic and copies ran while one was open for 0% of the time, Pallas kernels for 7%

profile of v5, /device:TPU:0, one launch (start us, length us, event | category | flops | bytes accessed | tf_op | source)
XLA Modules:
  0.0 134.9 jit_solution(11919071254057777759)
XLA Ops:
  0.0 2.4 %edges.1 = (f32[80,768]{1,0:T(8,128)}, f32[80,768]{1,0:T(8,128)}, f32[64,768]{1,0:T(8,128)}) custom-call(f32[8]{0:T(128)} %ks_far.1, f32[8]{0:T(128)} %alpha_far.1, f32[24,32,768]{2,1,0:T(8,128)} %heads_ref.3, s32[32,768]{1,0:T(8,128)} %soil_far.1), custom_call_target="tpu_custom_call" | custom-call | tf_op jit(solution)/shard_map/edges/pallas_call | solution.py:212
  2.4 1.3 collective-permute-start
  3.7 1.3 collective-permute-start.1
  6.0 9.4 %interior.1 = (f32[32,24,768]{2,1,0:T(8,128)}, f32[288,768]{1,0:T(8,128)S(1)}) custom-call(f32[24,32,768]{2,1,0:T(8,128)S(1)} %copy-done, f32[64,768]{1,0:T(8,128)S(1)} %copy-done.2), custom_call_target="tpu_custom_call" | custom-call | flops 60000000 | bytes 5000000 | tf_op jit(solution)/shard_map/interior/pallas_call | solution.py:226
  15.4 2.2 %edge.1 = f32[32,24,768]{2,1,0:T(8,128)} custom-call(f32[80,768]{1,0:T(8,128)S(1)} %collective-permute-done.above_ref, f32[80,768]{1,0:T(8,128)S(1)} %collective-permute-done.1.below_ref, f32[288,768]{1,0:T(8,128)S(1)} %get-tuple-element.15.saved_ref, f32[64,768]{1,0:T(8,128)S(1)} %copy-done.2, ...), custom_call_target="tpu_custom_call", output_to_operand_aliasing={{}: (4, {})} | custom-call | tf_op jit(solution)/shard_map/edge/pallas_call | solution.py:238
  17.6 6.5 %all-to-all-start = ((f32[8,4,24,768]{3,2,1,0:T(8,128)}), f32[8,4,24,768]{3,2,1,0:T(8,128)S(1)}, u32[]{:S(2)}, u32[]{:S(2)}) async-start(f32[8,4,24,768]{3,2,1,0:T(8,128)} %bitcast.2), calls=%async_computation | async-start | bytes 4718592 | tf_op jit(solution)/shard_map/all_to_all | solution.py:449
  24.2 34.9 %all-to-all-done.heads_ref = f32[8,4,24,768]{3,2,1,0:T(8,128)S(1)} async-done(((f32[8,4,24,768]{3,2,1,0:T(8,128)}), f32[8,4,24,768]{3,2,1,0:T(8,128)S(1)}, u32[]{:S(2)}, u32[]{:S(2)}) %all-to-all-start) | async-done | bytes 2359328 | tf_op jit(solution)/shard_map/all_to_all | solution.py:449
  59.1 2.1 %gram.1 = (f32[8,4,24,768]{3,2,1,0:T(8,128)S(1)}, f32[176,128]{1,0:T(8,128)S(1)}) custom-call(s32[4,6]{1,0:T(4,128)S(1)} %copy-done.3, f32[24,32,128]{2,1,0:T(8,128)S(1)} %bitcast.7, f32[32,24]{1,0:T(8,128)S(1)} %bitcast.8, f32[8,4,24,768]{3,2,1,0:T(8,128)S(1)} %all-to-all-done.heads_ref), custom_call_target="tpu_custom_call" | custom-call | tf_op jit(solution)/shard_map/gram/pallas_call | solution.py:357
  61.3 1.1 collective-permute-start.2
  64.3 2.4 %collective-permute-start.4 = (f32[88,128]{1,0:T(8,128)S(1)}, f32[88,128]{1,0:T(8,128)S(1)}, u32[]{:S(2)}, u32[]{:S(2)}) collective-permute-start(f32[88,128]{1,0:T(8,128)S(1)} %select_add_fusion), channel_id=1, source_target_pairs={{0,8},{1,9},{2,10},{3,11},{4,12},{5,13},{6,14},{7,15},{8,0},{9,1},... | collective-permute-start | bytes 135176 | tf_op jit(solution)/shard_map/ppermute | solution.py:283
  66.7 2.5 %collective-permute-start.5 = (f32[88,128]{1,0:T(8,128)S(1)}, f32[88,128]{1,0:T(8,128)S(1)}, u32[]{:S(2)}, u32[]{:S(2)}) collective-permute-start(f32[88,128]{1,0:T(8,128)S(1)} %select_add_fusion), channel_id=1, source_target_pairs={{0,24},{1,25},{2,26},{3,27},{4,28},{5,29},{6,30},{7,31},{8,16},{9,... | collective-permute-start | bytes 135176 | tf_op jit(solution)/shard_map/ppermute | solution.py:283
  69.8 1.1 collective-permute-done.5
  71.0 1.2 collective-permute-start.7
  72.2 2.0 %collective-permute-start.8 = (f32[88,128]{1,0:T(8,128)S(1)}, f32[88,128]{1,0:T(8,128)S(1)}, u32[]{:S(2)}, u32[]{:S(2)}) collective-permute-start(f32[88,128]{1,0:T(8,128)S(1)} %add_add_fusion.2), channel_id=1, source_target_pairs={{0,96},{16,112},{32,0},{48,16},{64,32},{80,48},{96,64},{112,80},{1... | collective-permute-start | bytes 135176 | tf_op jit(solution)/shard_map/ppermute | solution.py:283
  74.3 2.0 %collective-permute-done.6 = f32[88,128]{1,0:T(8,128)S(1)} collective-permute-done((f32[88,128]{1,0:T(8,128)S(1)}, f32[88,128]{1,0:T(8,128)S(1)}, u32[]{:S(2)}, u32[]{:S(2)}) %collective-permute-start.6) | collective-permute-done | bytes 45088 | tf_op jit(solution)/shard_map/ppermute | solution.py:283
  77.6 4.9 %collective-permute-start.10 = (f32[88,128]{1,0:T(8,128)S(1)}, f32[88,128]{1,0:T(8,128)S(1)}, u32[]{:S(2)}, u32[]{:S(2)}) collective-permute-start(f32[88,128]{1,0:T(8,128)S(1)} %add_add_fusion.1), channel_id=1, source_target_pairs={{0,4},{1,5},{2,6},{3,7},{4,0},{5,1},{6,2},{7,3},{8,12},{9,13},{10,... | collective-permute-start | bytes 135176 | tf_op jit(solution)/shard_map/ppermute | solution.py:283
  82.6 1.6 %collective-permute-start.11 = (f32[88,128]{1,0:T(8,128)S(1)}, f32[88,128]{1,0:T(8,128)S(1)}, u32[]{:S(2)}, u32[]{:S(2)}) collective-permute-start(f32[88,128]{1,0:T(8,128)S(1)} %add_add_fusion.1), channel_id=1, source_target_pairs={{0,6},{1,7},{2,0},{3,1},{4,2},{5,3},{6,4},{7,5},{8,14},{9,15},{10,... | collective-permute-start | bytes 135176 | tf_op jit(solution)/shard_map/ppermute | solution.py:283
  84.9 1.9 %collective-permute-done.11 = f32[88,128]{1,0:T(8,128)S(1)} collective-permute-done((f32[88,128]{1,0:T(8,128)S(1)}, f32[88,128]{1,0:T(8,128)S(1)}, u32[]{:S(2)}, u32[]{:S(2)}) %collective-permute-start.11) | collective-permute-done | bytes 45088 | tf_op jit(solution)/shard_map/ppermute | solution.py:283
  86.8 2.6 %collective-permute-done.9 = f32[88,128]{1,0:T(8,128)S(1)} collective-permute-done((f32[88,128]{1,0:T(8,128)S(1)}, f32[88,128]{1,0:T(8,128)S(1)}, u32[]{:S(2)}, u32[]{:S(2)}) %collective-permute-start.9) | collective-permute-done | bytes 45088 | tf_op jit(solution)/shard_map/ppermute | solution.py:283
  89.5 1.2 collective-permute-done.12
  90.8 7.1 %newton.1.weights_ref = f32[192,192]{1,0:T(8,128)S(1)} custom-call(f32[176,128]{1,0:T(8,128)S(1)} %pad_maximum_fusion.packed_ref), custom_call_target="tpu_custom_call" | custom-call | tf_op jit(solution)/shard_map/newton/pallas_call | solution.py:410
  97.9 1.1 mix.1
  99.0 33.8 %all_to_all.10 = f32[8,4,24,768]{3,2,1,0:T(8,128)S(1)} all-to-all(f32[8,4,24,768]{3,2,1,0:T(8,128)S(1)} %mix.1), channel_id=1, replica_groups=mesh['group'=8,'dev'=16] {'group'}, dimensions={0} | all-to-all | bytes 4718592 | tf_op jit(solution)/shard_map/all_to_all | solution.py:454
  132.8 2.1 %copy.15 = f32[32,24,768]{2,0,1:T(8,128)} copy(f32[32,24,768]{2,1,0:T(8,128)S(1)} %bitcast.9) | data formatting | bytes 4718592 | tf_op jit(solution)/shard_map/reshape | solution.py:455
  (32 shorter events, 5.8 us)
Async XLA Ops:
  0.0 5.0 %copy-start = (f32[24,32,768]{2,1,0:T(8,128)S(1)}, f32[24,32,768]{2,1,0:T(8,128)}, u32[]{:S(2)}) copy-start(f32[24,32,768]{2,1,0:T(8,128)} %heads_ref.3) | copy-start | bytes 7077892
  2.4 12.9 %collective-permute-start = (f32[80,768]{1,0:T(8,128)}, f32[80,768]{1,0:T(8,128)S(1)}, u32[]{:S(2)}, u32[]{:S(2)}) collective-permute-start(f32[80,768]{1,0:T(8,128)} %get-tuple-element.12), channel_id=1, source_target_pairs={{0,1},{1,2},{2,3},{3,4},{4,5},{5,6},{6,7},{7,8},{8,9},{9,10},{10,1... | collective-permute-start | bytes 737288 | tf_op jit(solution)/shard_map/ppermute | solution.py:222
  3.7 11.6 %collective-permute-start.1 = (f32[80,768]{1,0:T(8,128)}, f32[80,768]{1,0:T(8,128)S(1)}, u32[]{:S(2)}, u32[]{:S(2)}) collective-permute-start(f32[80,768]{1,0:T(8,128)} %get-tuple-element.13), channel_id=1, source_target_pairs={{1,0},{2,1},{3,2},{4,3},{5,4},{6,5},{7,6},{8,7},{9,8},{10,9},{11,1... | collective-permute-start | bytes 737288 | tf_op jit(solution)/shard_map/ppermute | solution.py:223
  5.0 0.9 copy-start.2
  17.6 6.5 %copy-start.4 = (f32[4,6,32]{2,0,1:T(4,128)S(1)}, f32[4,6,32]{2,0,1:T(4,128)}, u32[]{:S(2)}) copy-start(f32[4,6,32]{2,0,1:T(4,128)} %param.13) | copy-start | bytes 9220
  17.6 41.5 %copy-start.1 = (f32[4,6,32,128]{3,2,1,0:T(8,128)S(1)}, f32[4,6,32,128]{3,2,1,0:T(8,128)}, u32[]{:S(2)}) copy-start(f32[4,6,32,128]{3,2,1,0:T(8,128)} %param.11) | copy-start | bytes 1179652
  17.6 41.5 %copy-start.3 = (s32[4,6]{1,0:T(4,128)S(1)}, s32[4,6]{1,0:T(4,128)}, u32[]{:S(2)}) copy-start(s32[4,6]{1,0:T(4,128)} %mask_ref.1) | copy-start | bytes 292
  17.6 41.5 %all-to-all-start = ((f32[8,4,24,768]{3,2,1,0:T(8,128)}), f32[8,4,24,768]{3,2,1,0:T(8,128)S(1)}, u32[]{:S(2)}, u32[]{:S(2)}) async-start(f32[8,4,24,768]{3,2,1,0:T(8,128)} %bitcast.2), calls=%async_computation | async-start | bytes 4718592 | tf_op jit(solution)/shard_map/all_to_all | solution.py:449
  61.3 2.0 %collective-permute-start.2 = (f32[88,128]{1,0:T(8,128)S(1)}, f32[88,128]{1,0:T(8,128)S(1)}, u32[]{:S(2)}, u32[]{:S(2)}) collective-permute-start(f32[88,128]{1,0:T(8,128)S(1)} %slice_select_fusion), channel_id=1, source_target_pairs={{0,1},{1,0},{2,3},{3,2},{4,5},{5,4},{6,7},{7,6},{8,9},{9,8},{10,11... | collective-permute-start | bytes 135176 | tf_op jit(solution)/shard_map/ppermute | solution.py:271
  63.3 5.9 %collective-permute-start.3 = (f32[88,128]{1,0:T(8,128)S(1)}, f32[88,128]{1,0:T(8,128)S(1)}, u32[]{:S(2)}, u32[]{:S(2)}) collective-permute-start(f32[88,128]{1,0:T(8,128)S(1)} %select_add_fusion), channel_id=1, source_target_pairs={{0,16},{1,17},{2,18},{3,19},{4,20},{5,21},{6,22},{7,23},{8,24},{9,... | collective-permute-start | bytes 135176 | tf_op jit(solution)/shard_map/ppermute | solution.py:283
  64.3 5.6 %collective-permute-start.4 = (f32[88,128]{1,0:T(8,128)S(1)}, f32[88,128]{1,0:T(8,128)S(1)}, u32[]{:S(2)}, u32[]{:S(2)}) collective-permute-start(f32[88,128]{1,0:T(8,128)S(1)} %select_add_fusion), channel_id=1, source_target_pairs={{0,8},{1,9},{2,10},{3,11},{4,12},{5,13},{6,14},{7,15},{8,0},{9,1},... | collective-permute-start | bytes 135176 | tf_op jit(solution)/shard_map/ppermute | solution.py:283
  66.7 4.3 %collective-permute-start.5 = (f32[88,128]{1,0:T(8,128)S(1)}, f32[88,128]{1,0:T(8,128)S(1)}, u32[]{:S(2)}, u32[]{:S(2)}) collective-permute-start(f32[88,128]{1,0:T(8,128)S(1)} %select_add_fusion), channel_id=1, source_target_pairs={{0,24},{1,25},{2,26},{3,27},{4,28},{5,29},{6,30},{7,31},{8,16},{9,... | collective-permute-start | bytes 135176 | tf_op jit(solution)/shard_map/ppermute | solution.py:283
  71.0 5.3 %collective-permute-start.6 = (f32[88,128]{1,0:T(8,128)S(1)}, f32[88,128]{1,0:T(8,128)S(1)}, u32[]{:S(2)}, u32[]{:S(2)}) collective-permute-start(f32[88,128]{1,0:T(8,128)S(1)} %add_add_fusion.2), channel_id=1, source_target_pairs={{0,32},{16,48},{32,64},{48,80},{64,96},{80,112},{96,0},{112,16},{1... | collective-permute-start | bytes 135176 | tf_op jit(solution)/shard_map/ppermute | solution.py:283
  71.0 5.7 %collective-permute-start.7 = (f32[88,128]{1,0:T(8,128)S(1)}, f32[88,128]{1,0:T(8,128)S(1)}, u32[]{:S(2)}, u32[]{:S(2)}) collective-permute-start(f32[88,128]{1,0:T(8,128)S(1)} %add_add_fusion.2), channel_id=1, source_target_pairs={{0,64},{16,80},{32,96},{48,112},{64,0},{80,16},{96,32},{112,48},{1... | collective-permute-start | bytes 135176 | tf_op jit(solution)/shard_map/ppermute | solution.py:283
  72.2 5.4 %collective-permute-start.8 = (f32[88,128]{1,0:T(8,128)S(1)}, f32[88,128]{1,0:T(8,128)S(1)}, u32[]{:S(2)}, u32[]{:S(2)}) collective-permute-start(f32[88,128]{1,0:T(8,128)S(1)} %add_add_fusion.2), channel_id=1, source_target_pairs={{0,96},{16,112},{32,0},{48,16},{64,32},{80,48},{96,64},{112,80},{1... | collective-permute-start | bytes 135176 | tf_op jit(solution)/shard_map/ppermute | solution.py:283
  77.6 7.3 %collective-permute-start.10 = (f32[88,128]{1,0:T(8,128)S(1)}, f32[88,128]{1,0:T(8,128)S(1)}, u32[]{:S(2)}, u32[]{:S(2)}) collective-permute-start(f32[88,128]{1,0:T(8,128)S(1)} %add_add_fusion.1), channel_id=1, source_target_pairs={{0,4},{1,5},{2,6},{3,7},{4,0},{5,1},{6,2},{7,3},{8,12},{9,13},{10,... | collective-permute-start | bytes 135176 | tf_op jit(solution)/shard_map/ppermute | solution.py:283
  82.6 4.2 %collective-permute-start.11 = (f32[88,128]{1,0:T(8,128)S(1)}, f32[88,128]{1,0:T(8,128)S(1)}, u32[]{:S(2)}, u32[]{:S(2)}) collective-permute-start(f32[88,128]{1,0:T(8,128)S(1)} %add_add_fusion.1), channel_id=1, source_target_pairs={{0,6},{1,7},{2,0},{3,1},{4,2},{5,3},{6,4},{7,5},{8,14},{9,15},{10,... | collective-permute-start | bytes 135176 | tf_op jit(solution)/shard_map/ppermute | solution.py:283
  84.2 5.3 %collective-permute-start.9 = (f32[88,128]{1,0:T(8,128)S(1)}, f32[88,128]{1,0:T(8,128)S(1)}, u32[]{:S(2)}, u32[]{:S(2)}) collective-permute-start(f32[88,128]{1,0:T(8,128)S(1)} %add_add_fusion.1), channel_id=1, source_target_pairs={{0,2},{1,3},{2,4},{3,5},{4,6},{5,7},{6,0},{7,1},{8,10},{9,11},{10,... | collective-permute-start | bytes 135176 | tf_op jit(solution)/shard_map/ppermute | solution.py:283
  89.4 1.3 collective-permute-start.12
